TPU v7x, 128 devices: a whole 4x4x4 slice. The times are simulated.
128 devices in a mesh: image: 8 (over x_hi, y), patch: 16 (over x_lo, z, core).
Axes of the slice: x: 4 (x_hi: 2, x_lo: 2; x = x_hi * 2 + x_lo), y: 4, z: 4, core: 2. Of those that a mesh axis runs over, the one named last changes fastest.
Arguments:
- images: bfloat16 [8, 128, 64, 640], P('image', 'patch'), may hold values from -8 to 8
- heights: int32 [8], P('image'), may hold values from 8 to 128, as said below
- opening_scale_vector: float32 [640], replicated, may hold values from 0.25 to 1.75
- opening_offset_vector: float32 [640], replicated, may hold values from -3 to 3
- conv_weight: bfloat16 [3, 3, 640, 640], P(None, None, 'image'), may hold values from -0.078125 to 0.078125
- kernel_offset_vector: float32 [640], replicated, may hold values from -3 to 3
- closing_scale_vector: float32 [640], replicated, may hold values from 0.25 to 1.75
- closing_offset_vector: float32 [640], replicated, may hold values from -3 to 3
- query_weight: bfloat16 [640, 640], replicated, may hold values from -1 to 1
- key_weight: bfloat16 [640, 640], replicated, may hold values from -1 to 1
- value_weight: bfloat16 [640, 640], replicated, may hold values from -0.25 to 0.25
- out_weight: bfloat16 [640, 640], replicated, may hold values from -0.25 to 0.25
- out_bias: float32 [640], replicated, may hold values from -3 to 3
Outputs:
- block_features: bfloat16 [8, 128, 64, 640], P('image', 'patch')
Inputs may be any that keep to these rules, and one draw needn't show every extreme that they name: `heights`: every image uses at least 8 rows; in every batch some image uses all 128 rows.
All inputs are finite; a program needn't handle non-finite values.
Results may differ from a plain program's by a relative error of at most 0.0124.
The roundings to bfloat16 on the way count: a program that leaves them out, or rounds other values in their place, can miss the bound.
Values may be sent and summed in bfloat16 or wider, within the bound.
No kernel may reach another device: no remote copies, remote signals or barrier semaphores. Data moves between devices by JAX's collectives and lax.ppermute only.
A program may use at most 384 MiB of HBM per device.

v0:
```python
import jax
import jax.numpy as jnp
from jax import lax
from jax.sharding import PartitionSpec as P

HEAD_DIM = 64
GROUPS = 32


def padded_2(cells, sides, width):
    for axis, dim in sides:
        count = lax.axis_size(axis)
        ends = count - 1
        head = lax.slice_in_dim(cells, 0, width, axis=dim)
        tail = lax.slice_in_dim(cells, cells.shape[dim] - width, cells.shape[dim], axis=dim)
        cells = jnp.concatenate(
            [
                lax.ppermute(tail, axis, [(i, (i + 1) % count) for i in range(ends)]),
                cells,
                lax.ppermute(head, axis, [((i + 1) % count, i) for i in range(ends)]),
            ],
            axis=dim,
        )
    return cells


def normalize_rows(values, occupied_flags, gain, shift, entries_number):
    pixel_down, pixel_across, feature_depth = values.shape
    grouped = values.reshape(pixel_down, pixel_across, GROUPS, feature_depth // GROUPS)
    weight = occupied_flags.astype(jnp.float32)[:, None, None, None]
    mean = lax.psum(jnp.sum(grouped * weight, axis=(0, 1, 3)), "patch") / entries_number
    centred = (grouped - mean[None, None, :, None]) * weight
    spread = lax.psum(jnp.sum(centred * centred, axis=(0, 1, 3)), "patch") / entries_number
    scaled = (grouped - mean[None, None, :, None]) * lax.rsqrt(spread + 1e-05)[None, None, :, None]
    return scaled.reshape(pixel_down, pixel_across, feature_depth) * gain + shift


def per_device(
    images,
    heights,
    opening_scale_vector,
    opening_offset_vector,
    conv_weight,
    kernel_offset_vector,
    closing_scale_vector,
    closing_offset_vector,
    query_weight,
    key_weight,
    value_weight,
    out_weight,
    out_bias,
):
    kernel_neighbourhood = images[0]
    pixel_down, pixel_across, feature_depth = kernel_neighbourhood.shape
    tokens = pixel_down * pixel_across
    heads = feature_depth // HEAD_DIM
    height = heights[0]
    row_ids = lax.axis_index("patch") * pixel_down + jnp.arange(pixel_down, dtype=jnp.int32)
    occupied_flags = row_ids < height
    line_occupancy = occupied_flags.astype(jnp.float32)[:, None, None]
    entries_number = (height * pixel_across * (feature_depth // GROUPS)).astype(jnp.float32)
    window_beginning = kernel_neighbourhood.astype(jnp.float32) * line_occupancy
    opening_result = (
        jax.nn.silu(
            normalize_rows(
                window_beginning,
                occupied_flags,
                opening_scale_vector,
                opening_offset_vector,
                entries_number,
            )
        )
        * line_occupancy
    ).astype(jnp.bfloat16)
    rimmed = padded_2(opening_result, (("patch", 0),), 1)
    padded = jnp.pad(rimmed, ((0, 0), (1, 1), (0, 0)))
    cumulative_summed = jnp.zeros((tokens, feature_depth), jnp.float32)
    piece = lax.all_gather(conv_weight, "image", axis=2, tiled=True)
    width_in = piece.shape[2]
    for step_y in range(3):
        for step_x in range(3):
            window = padded[step_y : step_y + pixel_down, step_x : step_x + pixel_across].reshape(
                tokens, width_in
            )
            cumulative_summed = cumulative_summed + jnp.dot(
                window, piece[step_y, step_x], preferred_element_type=jnp.float32
            )
    spatial_filter_picture = cumulative_summed
    skip_source = (
        (
            window_beginning
            + spatial_filter_picture.reshape(pixel_down, pixel_across, feature_depth)
            + kernel_offset_vector
        )
        * line_occupancy
    ).astype(jnp.bfloat16)
    closing_result = (
        normalize_rows(
            skip_source.astype(jnp.float32),
            occupied_flags,
            closing_scale_vector,
            closing_offset_vector,
            entries_number,
        )
        * line_occupancy
    ).astype(jnp.bfloat16)
    flat = closing_result.reshape(tokens, feature_depth)
    query = jnp.dot(flat, query_weight, preferred_element_type=jnp.float32).astype(jnp.bfloat16)
    query_heads = query.reshape(tokens, heads, HEAD_DIM)
    scale = HEAD_DIM ** (-0.5)
    keys = jnp.dot(flat, key_weight, preferred_element_type=jnp.float32).astype(jnp.bfloat16)
    values = jnp.dot(flat, value_weight, preferred_element_type=jnp.float32).astype(jnp.bfloat16)
    absorb_keys = lax.all_gather(keys, "patch", axis=0, tiled=True)
    absorb_values = lax.all_gather(values, "patch", axis=0, tiled=True)
    top = jnp.full((heads, tokens), -1e30, jnp.float32)
    count_k = absorb_keys.shape[0]
    scores = (
        jnp.einsum(
            "qhd,khd->hqk",
            query_heads,
            absorb_keys.reshape(count_k, heads, HEAD_DIM),
            preferred_element_type=jnp.float32,
        )
        * scale
    )
    key_live = jnp.arange(count_k, dtype=jnp.int32) // pixel_across < height
    scores = jnp.where(key_live[None, None, :], scores, -1e30)
    new_top = jnp.maximum(top, jnp.max(scores, axis=-1))
    weights = jnp.exp(scores - new_top[:, :, None])
    cumulative_summed = jnp.sum(weights, axis=-1)
    update = jnp.einsum(
        "hqk,khd->qhd",
        weights.astype(jnp.bfloat16),
        absorb_values.reshape(count_k, heads, HEAD_DIM),
        preferred_element_type=jnp.float32,
    )
    acc = update
    top, cumulative_summed, acc = (new_top, cumulative_summed, acc)
    safe_total = jnp.where(cumulative_summed > 0.0, cumulative_summed, 1.0)
    mixed = (
        (acc / jnp.transpose(safe_total)[:, :, None])
        .reshape(tokens, feature_depth)
        .astype(jnp.bfloat16)
    )
    block_features = skip_source.astype(jnp.float32).reshape(tokens, feature_depth)
    block_features = (
        block_features + jnp.dot(mixed, out_weight, preferred_element_type=jnp.float32) + out_bias
    )
    block_features = (
        block_features.reshape(pixel_down, pixel_across, feature_depth) * line_occupancy
    )
    return block_features.astype(jnp.bfloat16)[None]


def solution(mesh):
    in_specs = (
        P("image", "patch", None, None),
        P("image"),
        P(),
        P(),
        P(None, None, "image", None),
        P(),
        P(),
        P(),
        P(),
        P(),
        P(),
        P(),
        P(),
    )
    out_specs = P("image", "patch", None, None)
    return jax.shard_map(
        per_device, mesh=mesh, in_specs=in_specs, out_specs=out_specs, check_vma=False
    )
```

profile of v0, /device:TPU:1, one launch (start us, length us, event | category | flops | bytes accessed | tf_op | source)
XLA Modules:
  0.0 448.1 jit_solution(2604334799893437484)
XLA Ops:
  8.5 29.4 %psum.28 = f32[32]{0:T(128)S(1)} all-reduce(f32[32]{0:T(128)S(1)} %reduce_sum.60), channel_id=1, replica_groups=mesh['image'=8,'patch'=16] {'patch'}, use_global_device_ids=true, to_apply=%region_2.0 | all-reduce | flops 32 | bytes 256 | tf_op jit(solution)/shard_map/psum | solution.py:31
  38.6 30.6 %psum.29 = f32[32]{0:T(128)S(1)} all-reduce(f32[32]{0:T(128)S(1)} %reduce_sum.66), channel_id=1, replica_groups=mesh['image'=8,'patch'=16] {'patch'}, use_global_device_ids=true, to_apply=%region_5.6 | all-reduce | flops 32 | bytes 256 | tf_op jit(solution)/shard_map/psum | solution.py:33
  70.7 1.9 collective-permute-start
  72.7 2.4 collective-permute-start.1
  75.2 1.4 multiply_convert_fusion.1
  76.9 2.2 collective-permute-done.1
  79.0 1.9 pad_maximum_fusion
  81.0 1.1 fusion.33
  82.1 1.8 fusion.47
  83.9 26.7 %all-gather.4.cloned.1.call-done = bf16[3,3,640,640]{3,2,1,0:T(8,128)(2,1)} async-done(((bf16[3,3,80,640]{3,2,1,0:T(8,128)(2,1)}), bf16[3,3,640,640]{3,2,1,0:T(8,128)(2,1)}) %all-gather.4.cloned.1.call-update) | async-done | bytes 7372816 | tf_op jit(solution)/shard_map/all_gather | solution.py:78
  110.6 2.2 fusion.35
  112.8 2.4 fusion.34
  115.2 2.0 convolution_add_fusion.6
  123.5 27.6 %psum.30 = f32[32]{0:T(128)S(1)} all-reduce(f32[32]{0:T(128)S(1)} %reduce_sum.83), channel_id=1, replica_groups=mesh['image'=8,'patch'=16] {'patch'}, use_global_device_ids=true, to_apply=%region_8.9 | all-reduce | flops 32 | bytes 256 | tf_op jit(solution)/shard_map/psum | solution.py:31
  151.7 29.1 %psum.31 = f32[32]{0:T(128)S(1)} all-reduce(f32[32]{0:T(128)S(1)} %reduce_sum.86), channel_id=1, replica_groups=mesh['image'=8,'patch'=16] {'patch'}, use_global_device_ids=true, to_apply=%region_11.12 | all-reduce | flops 32 | bytes 256 | tf_op jit(solution)/shard_map/psum | solution.py:33
  181.1 1.7 convolution_convert_fusion
  183.0 1.7 convolution_convert_fusion.2
  184.8 2.0 convolution_convert_fusion.1
  187.0 54.8 %all-gather.8.cloned.1.call-done = bf16[8192,640]{1,0:T(8,128)(2,1)} async-done(((bf16[512,640]{1,0:T(8,128)(2,1)}), bf16[8192,640]{1,0:T(8,128)(2,1)}) %all-gather.8.cloned.1.call-update) | async-done | bytes 10485776 | tf_op jit(solution)/shard_map/all_gather | solution.py:113
  241.8 14.5 %copy.19 = bf16[8192,640]{0,1:T(8,128)(2,1)} copy(bf16[8192,640]{1,0:T(8,128)(2,1)} %all-gather.8.cloned.1.call-done) | data formatting | bytes 20971520 | tf_op jit(solution)/shard_map/all_gather | solution.py:113
  256.3 60.9 %fusion = (f32[10,512]{1,0:T(8,128)S(1)}, f32[10,512,8192]{2,1,0:T(8,128)}) fusion(pred[8192]{0:T(1024)(128)(4,1)S(1)} %fusion.36, bf16[512,10,64]{0,2,1:T(8,128)(2,1)S(1)} %bitcast.95, bf16[8192,10,64]{0,2,1:T(8,128)(2,1)} %bitcast.84), kind=kOutput, calls=%fused_computation.2 | convolution fusion | flops 5494533120 | bytes 178941952 | tf_op jit(solution)/shard_map/qhd,khd->hqk/dot_general | solution.py:118
  317.2 51.2 %fusion.1 = f32[10,512]{1,0:T(8,128)S(1)} fusion(f32[10,512,8192]{2,1,0:T(8,128)} %get-tuple-element.18, f32[10,512]{1,0:T(8,128)S(1)} %broadcast_maximum_fusion, pred[8192]{0:T(1024)(128)(4,1)S(1)} %fusion.36), kind=kLoop, calls=%fused_computation.3 | loop fusion | flops 167767040 | bytes 167821312 | tf_op jit(solution)/shard_map/reduce_sum | solution.py:130
  368.5 14.5 %copy.17 = bf16[8192,640]{0,1:T(8,128)(2,1)} copy(bf16[8192,640]{1,0:T(8,128)(2,1)} %all-gather.6.cloned.1.call-done) | data formatting | bytes 20971520 | tf_op jit(solution)/shard_map/all_gather | solution.py:114
  383.0 56.7 %divide_convert_fusion = bf16[512,10,64]{0,2,1:T(8,128)(2,1)S(1)} fusion(f32[512,10]{0,1:T(8,128)S(1)} %compare_select_fusion, bf16[8192,10,64]{0,2,1:T(8,128)(2,1)} %bitcast.85, f32[10,512,8192]{2,1,0:T(8,128)} %get-tuple-element.18, f32[10,512]{1,0:T(8,128)S(1)} %broadcast_maximum_fusion, pred[8192]{0:T(1024)(128)(4,1)S(1)} %fusion.36), kind=kOutput, calls=%fused_computation.46 | convolution fusion | flops 5537136640 | bytes 178962432 | tf_op jit(solution)/shard_map/hqk,khd->qhd/dot_general | solution.py:131
  (91 shorter events, 13.2 us)
Async XLA Ops:
  6.5 174.5 %copy-start = (bf16[640,640]{1,0:T(8,128)(2,1)S(1)}, bf16[640,640]{1,0:T(8,128)(2,1)}, u32[]{:S(2)}) copy-start(bf16[640,640]{1,0:T(8,128)(2,1)} %param.22) | copy-start | bytes 2457604
  6.5 1.4 copy-start.2
  6.5 62.9 %copy-start.14 = (f32[640]{0:T(1024)S(1)}, f32[640]{0:T(1024)}, u32[]{:S(2)}) copy-start(f32[640]{0:T(1024)} %param.15) | copy-start | bytes 7684
  6.5 62.9 %copy-start.13 = (f32[640]{0:T(1024)S(1)}, f32[640]{0:T(1024)}, u32[]{:S(2)}) copy-start(f32[640]{0:T(1024)} %param.16) | copy-start | bytes 7684
  6.5 104.1 %all-gather.4.cloned.1.call-start = ((), (), s32[]{:S(2)}) async-start(), calls=%async_computation | async-start | bytes 8294400 | tf_op jit(solution)/shard_map/all_gather | solution.py:78
  7.3 234.6 %all-gather.8.cloned.1.call-start = ((), (), s32[]{:S(2)}) async-start(), calls=%async_computation.2 | async-start | bytes 11141120 | tf_op jit(solution)/shard_map/all_gather | solution.py:113
  8.0 67.2 %copy-start.11 = (f32[8]{0:T(128)}, f32[8]{0:T(128)S(1)}, u32[]{:S(2)}) copy-start(f32[8]{0:T(128)S(1)} %compare_convert_fusion) | copy-start | bytes 100
  70.7 6.1 %collective-permute-start = (bf16[1,64,640]{2,1,0:T(8,128)(2,1)}, bf16[1,64,640]{2,1,0:T(8,128)(2,1)S(1)}, u32[]{:S(2)}, u32[]{:S(2)}) collective-permute-start(bf16[1,64,640]{2,1,0:T(8,128)(2,1)} %get-tuple-element.13), channel_id=1, source_target_pairs={{0,1},{1,2},{2,3},{3,4},{4,5},{5,6},{6,7},{7,8},{8,9},{9,10},{10,1... | collective-permute-start | bytes 245768 | tf_op jit(solution)/shard_map/ppermute | solution.py:18
  72.7 6.4 %collective-permute-start.1 = (bf16[1,64,640]{2,1,0:T(8,128)(2,1)}, bf16[1,64,640]{2,1,0:T(8,128)(2,1)}, u32[]{:S(2)}, u32[]{:S(2)}) collective-permute-start(bf16[1,64,640]{2,1,0:T(8,128)(2,1)} %get-tuple-element.14), channel_id=1, source_target_pairs={{1,0},{2,1},{3,2},{4,3},{5,4},{6,5},{7,6},{8,7},{9,8},{10,9},{11,1... | collective-permute-start | bytes 245768 | tf_op jit(solution)/shard_map/ppermute | solution.py:20
  110.6 6.6 %copy-start.3 = (bf16[3,3,640,640]{3,2,1,0:T(8,128)(2,1)S(1)}, bf16[3,3,640,640]{3,2,1,0:T(8,128)(2,1)}, u32[]{:S(2)}) copy-start(bf16[3,3,640,640]{3,2,1,0:T(8,128)(2,1)} %all-gather.4.cloned.1.call-done) | copy-start | bytes 22118404
  115.2 2.0 copy-start.7
  117.2 1.1 copy-start.6
  118.3 1.1 copy-start.4
  119.4 1.1 copy-start.5
  121.2 1.1 copy-start.8
  122.3 58.7 %copy-start.18 = (f32[640]{0:T(1024)S(1)}, f32[640]{0:T(1024)}, u32[]{:S(2)}) copy-start(f32[640]{0:T(1024)} %param.20) | copy-start | bytes 7684
  122.3 58.7 %copy-start.19 = (f32[640]{0:T(1024)S(1)}, f32[640]{0:T(1024)}, u32[]{:S(2)}) copy-start(f32[640]{0:T(1024)} %param.19) | copy-start | bytes 7684
  123.2 61.5 %copy-start.9 = (bf16[512,640]{1,0:T(8,128)(2,1)}, bf16[512,640]{1,0:T(8,128)(2,1)S(1)}, u32[]{:S(2)}) copy-start(bf16[512,640]{1,0:T(8,128)(2,1)S(1)} %get-tuple-element.16) | copy-start | bytes 1966084
  181.1 1.9 copy-start.16
  182.8 185.7 %all-gather.6.cloned.1.call-start = ((), (), s32[]{:S(2)}) async-start(), calls=%async_computation.1 | async-start | bytes 11141120 | tf_op jit(solution)/shard_map/all_gather | solution.py:114
  383.0 56.7 %copy-start.10 = (bf16[512,640]{1,0:T(8,128)(2,1)S(1)}, bf16[512,640]{1,0:T(8,128)(2,1)}, u32[]{:S(2)}) copy-start(bf16[512,640]{1,0:T(8,128)(2,1)} %copy-done.9) | copy-start | bytes 1966084
  383.0 56.7 %copy-start.17 = (bf16[640,640]{1,0:T(8,128)(2,1)S(1)}, bf16[640,640]{1,0:T(8,128)(2,1)}, u32[]{:S(2)}) copy-start(bf16[640,640]{1,0:T(8,128)(2,1)} %param.24) | copy-start | bytes 2457604
  383.0 56.7 %copy-start.20 = (f32[640]{0:T(1024)S(1)}, f32[640]{0:T(1024)}, u32[]{:S(2)}) copy-start(f32[640]{0:T(1024)} %param.25) | copy-start | bytes 7684
  439.7 1.8 copy-start.1
  (2 other events, 1.9 us)
Sparse Core Ops, SparseCore 0:
  9.8 100.7 all-gather.3
  182.9 58.9 all-gather.7
  243.5 62.9 all-gather.5
where the time goes:
time: 449 us; the launch traced here: 448 us
  matrix products  135 us (30%)
  blocking collectives  117 us (26%)
  waiting for transfers between devices  84.4 us (19%)
  other arithmetic  58.9 us (13%)
  local copies, waits for them, and re-layouts  34.2 us (8%)
  between operations  14.2 us (3%)
  starting transfers between devices  4.61 us (1%)
    dot_general x1, matrix products, per_device(): jnp.einsum('qhd,khd->hqk', query_heads, absorb_keys.reshape(count_k, head...  60.9 us
    psum x2, blocking collectives, normalize_rows(): lax.psum(jnp.sum(centred * centred, axis=(0, 1, 3)), 'patch')  59.7 us
    psum x2, blocking collectives, normalize_rows(): lax.psum(jnp.sum(grouped * weight, axis=(0, 1, 3)), 'patch')  57 us
    dot_general x1, matrix products, per_device(): jnp.einsum('hqk,khd->qhd', weights.astype(jnp.bfloat16), absorb_values.re...  56.7 us
    all_gather x1, waiting for transfers between devices, per_device(): absorb_keys = lax.all_gather(keys, 'patch', axis=0, tiled=True)  54.8 us
    reduce_sum x1, other arithmetic, per_device(): cumulative_summed = jnp.sum(weights, axis=-1)  51.2 us
    all_gather x1, waiting for transfers between devices, per_device(): piece = lax.all_gather(conv_weight, 'image', axis=2, tiled=True)  26.7 us
    all_gather x1, local copies, waits for them, and re-layouts, per_device(): absorb_values = lax.all_gather(values, 'patch', axis=0, tiled=True)  14.5 us
  transfers between devices with their start and end apart: 5, of which 3 were waited for; matrix products, arithmetic and copies ran while one was open for 31% of the time, Pallas kernels for 0%

commit v1 on v0

v1 whole, which is shorter than its diff:
```python
import functools

import jax
import jax.numpy as jnp
from jax import lax
from jax.experimental import pallas as pl
from jax.experimental.pallas import tpu as pltpu
from jax.sharding import PartitionSpec as P

HEAD_DIM = 64
GROUPS = 32
C = 640
W = 64
RP = 8
TOK = RP * W
HEADS = C // HEAD_DIM
PAIRS = HEADS // 2
VROWS = 80
HALF = 368
BOTH = ("image", "patch")
SCORE_SCALE = HEAD_DIM**-0.5 * 1.4426950408889634
VMEM = pl.BlockSpec(memory_space=pltpu.VMEM)
SMEM = pl.BlockSpec(memory_space=pltpu.SMEM)
ANY = pl.BlockSpec(memory_space=pl.ANY)
F32 = jnp.float32
BF16 = jnp.bfloat16


def params(mib):
    return pltpu.CompilerParams(vmem_limit_bytes=mib << 20)


def shape(dims, kind):
    return jax.ShapeDtypeStruct(dims, kind)


def pairs_of(move):
    pairs = []
    for x in range(4):
        for y in range(4):
            for z in range(4):
                for core in range(2):
                    ends = []
                    for a, b, c, d in ((x, y, z, core), move(x, y, z, core)):
                        a, b, c = a % 4, b % 4, c % 4
                        ends.append((a // 2 * 4 + b) * 16 + a % 2 * 8 + c * 2 + d)
                    pairs.append(tuple(ends))
    return pairs


SIBLING = pairs_of(lambda x, y, z, core: (x, y, z, 1 - core))
Y_UP = pairs_of(lambda x, y, z, core: (x, y + 1, z, core))
Y_DOWN = pairs_of(lambda x, y, z, core: (x, y - 1, z, core))
Z_UP = pairs_of(lambda x, y, z, core: (x, y, z + 1, core))
Z_DOWN = pairs_of(lambda x, y, z, core: (x, y, z - 1, core))
X_LO = pairs_of(lambda x, y, z, core: (x ^ 1, y, z, core))
X_HI = pairs_of(lambda x, y, z, core: (3 - x, y, z, core))


def send(block, pairs):
    return lax.ppermute(block, BOTH, pairs)


def row_live(count, first_row, height):
    rows = lax.broadcasted_iota(jnp.int32, (count, 1), 0) // W + first_row
    return jnp.where(jnp.logical_and(rows >= 0, rows < height), 1.0, 0.0)


def channel_stats(cells, live, live_count, out_ref):
    mean = jnp.sum(cells * live, axis=0, keepdims=True) / jnp.maximum(live_count, 1.0)
    centred = (cells - mean) * live
    out_ref[0:1, :] = mean
    out_ref[1:2, :] = jnp.sum(centred * centred, axis=0, keepdims=True)


def stats_kernel(place_ref, image_ref, out_ref):
    first_row, height = place_ref[0], place_ref[1]
    count = (jnp.clip(height - first_row, 0, RP) * W).astype(F32)
    channel_stats(image_ref[...].astype(F32), row_live(TOK, first_row, height), count, out_ref)


def activate_kernel(place_ref, image_ref, above_ref, below_ref, affine_ref, out_ref):
    first_row, height = place_ref[0], place_ref[1]
    mean, gain, shift = affine_ref[0:1, :], affine_ref[1:2, :], affine_ref[2:3, :]

    def put(at, count, block, row):
        live = row_live(count, row, height)
        v = (block.astype(F32) * live - mean) * gain + shift
        out_ref[at : at + count, :] = (v / (1.0 + jnp.exp(-v)) * live).astype(BF16)

    put(0, W, above_ref[...], first_row - 1)
    put(W, TOK, image_ref[...], first_row)
    put(W + TOK, W, below_ref[...], first_row + RP)


def conv_kernel(place_ref, first_ref, image_ref, bias_ref, own_ref, *refs):
    mine, theirs = refs[:7], refs[7:14]
    resid_ref, stats_ref, kernel, sem = refs[14:]
    first_row, height, core = place_ref[0], place_ref[1], place_ref[2]
    order = [dy * 3 + dx for dx in range(3) for dy in range(3)]

    def load(source, rows, count, tap, channel):
        pltpu.make_async_copy(
            source.at[pl.ds(rows, count), :],
            kernel.at[tap, pl.ds(pl.multiple_of(channel, 16), count), :],
            sem.at[tap],
        ).start()

    def load_all(lows, highs):
        for tap in order:
            for i in range(7):
                channel = place_ref[4 + i] * 80
                if tap <= 3:
                    load(lows[i], 80 * tap, 80, tap, channel)
                elif tap >= 5:
                    load(highs[i], 80 * tap - 352, 80, tap, channel)
                else:
                    load(lows[i], 320, 48, tap, channel)
                    load(highs[i], 16, 32, tap, channel + 48)

    for tap in order:
        load(own_ref, 80 * tap, 80, tap, place_ref[3] * 80)
    pl.when(core == 0)(lambda: load_all(mine, theirs))
    pl.when(core != 0)(lambda: load_all(theirs, mine))

    columns = lax.broadcasted_iota(jnp.int32, (TOK, 1), 0) % W
    total = None
    for dx in (0, 1, 2):
        part = None
        for dy in range(3):
            tap = dy * 3 + dx
            pltpu.make_async_copy(kernel.at[tap], kernel.at[tap], sem.at[tap]).wait()
            product = jnp.dot(
                first_ref[dy * W : dy * W + TOK, :], kernel[tap], preferred_element_type=F32
            )
            part = product if part is None else part + product
        if dx == 0:
            part = jnp.where(columns == 0, 0.0, pltpu.roll(part, 1, 0))
        if dx == 2:
            part = jnp.where(columns == W - 1, 0.0, pltpu.roll(part, TOK - 1, 0))
        total = part if total is None else total + part
    live = row_live(TOK, first_row, height)
    start = image_ref[...].astype(F32) * live
    resid = ((start + total + bias_ref[...]) * live).astype(BF16)
    resid_ref[...] = resid
    count = (jnp.clip(height - first_row, 0, RP) * W).astype(F32)
    channel_stats(resid.astype(F32), live, count, stats_ref)


def second_kernel(place_ref, resid_ref, affine_ref, out_ref):
    mean, gain, shift = affine_ref[0:1, :], affine_ref[1:2, :], affine_ref[2:3, :]
    live = row_live(TOK, place_ref[0], place_ref[1])
    v = (resid_ref[...].astype(F32) - mean) * gain + shift
    out_ref[...] = (v * live).astype(BF16)


def transposed(weight_t, block):
    return lax.dot_general(
        weight_t, block, (((1,), (1,)), ((), ())), preferred_element_type=F32
    ).astype(BF16)


def put_values(place_ref, at, weight_ref, block, n, values_ref):
    tokens = lax.broadcasted_iota(jnp.int32, (VROWS - HEAD_DIM, TOK), 1)
    lines = lax.broadcasted_iota(jnp.int32, (VROWS - HEAD_DIM, TOK), 0)
    rows = tokens // W + place_ref[at]
    ones = jnp.where(jnp.logical_and(lines == 0, rows < place_ref[1]), 1.0, 0.0).astype(BF16)
    values = transposed(weight_ref[...], block)
    span = slice(n * TOK, (n + 1) * TOK)
    for h in range(HEADS):
        values_ref[h, 0:HEAD_DIM, span] = values[h * HEAD_DIM : (h + 1) * HEAD_DIM]
        values_ref[h, HEAD_DIM:VROWS, span] = ones


def query_kernel(second_ref, wq_ref, out_ref):
    q = transposed(wq_ref[...], second_ref[...])
    zero = jnp.zeros((HEAD_DIM, TOK), BF16)
    for p in range(PAIRS):
        a = p * 2 * HEAD_DIM
        out_ref[p, 0:HEAD_DIM, 0:TOK] = q[a : a + HEAD_DIM]
        out_ref[p, 0:HEAD_DIM, TOK : 2 * TOK] = zero
        out_ref[p, HEAD_DIM : 2 * HEAD_DIM, 0:TOK] = zero
        out_ref[p, HEAD_DIM : 2 * HEAD_DIM, TOK : 2 * TOK] = q[a + HEAD_DIM : a + 2 * HEAD_DIM]


def project_kernel(sizes, place_ref, *refs):
    blocks = refs[: len(sizes)]
    wk_ref, wv_ref, keys_ref, values_ref, held = refs[len(sizes) :]
    at = 0
    for ref, size in zip(blocks, sizes):
        held[at : at + size, :] = ref[...]
        at += size
    for n in range(at // TOK):
        block = held[n * TOK : (n + 1) * TOK, :]
        keys_ref[n * TOK : (n + 1) * TOK, :] = jnp.dot(
            block, wk_ref[...], preferred_element_type=F32
        ).astype(BF16)
        put_values(place_ref, 2 + n, wv_ref, block, n, values_ref)


def open_kernel(query_ref, keys_ref, values_ref, acc_ref, top_ref):
    for p in range(PAIRS):
        span = slice(p * 2 * HEAD_DIM, (p + 1) * 2 * HEAD_DIM)
        s = jnp.dot(keys_ref[:, span], query_ref[p], preferred_element_type=F32) * SCORE_SCALE
        top = jnp.max(s, axis=0, keepdims=True)
        top_ref[p] = jnp.broadcast_to(top, (8, 2 * TOK))
        weights = jnp.exp2(s - top).astype(BF16)
        for h in range(2):
            acc_ref[2 * p + h] = jnp.dot(
                values_ref[2 * p + h],
                weights[:, h * TOK : (h + 1) * TOK],
                preferred_element_type=F32,
            )


def attend_kernel(query_ref, top_ref, keys_ref, values_ref, held_ref, acc_ref):
    @pl.when(pl.program_id(0) == 0)
    def _():
        acc_ref[...] = held_ref[...]

    for p in range(PAIRS):
        span = slice(p * 2 * HEAD_DIM, (p + 1) * 2 * HEAD_DIM)
        s = jnp.dot(keys_ref[:, span], query_ref[p], preferred_element_type=F32)
        weights = jnp.exp2(s * SCORE_SCALE - top_ref[p, 0:1, :]).astype(BF16)
        for h in range(2):
            acc_ref[2 * p + h] += jnp.dot(
                values_ref[2 * p + h],
                weights[:, h * TOK : (h + 1) * TOK],
                preferred_element_type=F32,
            )


def finish_kernel(place_ref, acc_ref, resid_ref, wo_ref, bias_ref, out_ref, far_ref):
    mixed = []
    far = jnp.zeros((1, TOK), F32)
    for h in range(HEADS):
        total = acc_ref[h, HEAD_DIM : HEAD_DIM + 1, :]
        inside = jnp.logical_and(total > 2.0**-60, total < 2.0**100)
        far = jnp.maximum(far, jnp.where(inside, 0.0, 1.0))
        mixed.append((acc_ref[h, 0:HEAD_DIM, :] / total).astype(BF16))
    far_ref[0, 0] = jnp.max(far).astype(jnp.int32)
    update = lax.dot_general(
        jnp.concatenate(mixed, axis=0),
        wo_ref[...],
        (((0,), (0,)), ((), ())),
        preferred_element_type=F32,
    )
    live = row_live(TOK, place_ref[0], place_ref[1])
    out_ref[...] = ((resid_ref[...].astype(F32) + update + bias_ref[...]) * live).astype(BF16)


def exact_attention(query, keys, values, resid, out_weight, out_bias, live):
    keys = jnp.concatenate(keys, axis=0)
    values = jnp.concatenate(values, axis=2)
    key_live = values[0, HEAD_DIM] > 0

    def one_head(h):
        q = lax.dynamic_slice(
            query, (h // 2, h % 2 * HEAD_DIM, h % 2 * TOK), (1, HEAD_DIM, TOK)
        )[0]
        k = lax.dynamic_slice(keys, (0, h * HEAD_DIM), (keys.shape[0], HEAD_DIM))
        v = lax.dynamic_slice(values, (h, 0, 0), (1, HEAD_DIM, keys.shape[0]))[0]
        s = jnp.dot(k, q, preferred_element_type=F32) * HEAD_DIM**-0.5
        s = jnp.where(key_live[:, None], s, -1e30)
        weights = jnp.exp(s - jnp.max(s, axis=0, keepdims=True))
        total = jnp.sum(weights, axis=0, keepdims=True)
        return (jnp.dot(v, weights.astype(BF16), preferred_element_type=F32) / total).astype(BF16)

    mixed = lax.map(one_head, jnp.arange(HEADS, dtype=jnp.int32)).reshape(C, TOK)
    update = lax.dot_general(
        mixed, out_weight, (((0,), (0,)), ((), ())), preferred_element_type=F32
    )
    return ((resid.astype(F32) + update + out_bias[None, :]) * live).astype(BF16)


def combine(stats, height, gain, shift):
    everyone = lax.all_to_all(
        jnp.broadcast_to(stats[None], (16,) + stats.shape), "patch", 0, 0, tiled=False
    )
    rows = jnp.clip(height - RP * jnp.arange(16, dtype=jnp.int32), 0, RP)
    counts = (rows * W).astype(F32)[:, None, None]
    entries = (height * W * (C // GROUPS)).astype(F32)
    means = everyone[:, 0].reshape(16, GROUPS, C // GROUPS)
    squares = everyone[:, 1].reshape(16, GROUPS, C // GROUPS)
    mean = jnp.sum(means * counts, axis=(0, 2)) / entries
    apart = means - mean[None, :, None]
    spread = jnp.sum(squares + counts * apart * apart, axis=(0, 2)) / entries
    scale = lax.rsqrt(spread + 1e-05)
    wide = lambda v: jnp.broadcast_to(v[:, None], (GROUPS, C // GROUPS)).reshape(C)
    return jnp.stack([wide(mean), wide(scale) * gain, shift])


def per_device(
    images,
    heights,
    opening_scale_vector,
    opening_offset_vector,
    conv_weight,
    kernel_offset_vector,
    closing_scale_vector,
    closing_offset_vector,
    query_weight,
    key_weight,
    value_weight,
    out_weight,
    out_bias,
):
    image = images[0].reshape(TOK, C)
    height = heights[0]
    at_image = lax.axis_index("image")
    at_patch = lax.axis_index("patch")
    core = at_patch % 2
    first_row = at_patch * RP
    place = jnp.stack([first_row, height])

    own = conv_weight.reshape(9 * 80, C)
    half = lax.dynamic_slice(own, (core * (720 - HALF), 0), (HALF, C))
    a_up = send(half, Y_UP)
    a_down = send(half, Y_DOWN)
    b_own = send(half, X_HI)
    up_pairs = [(g * 16 + i, g * 16 + i + 1) for g in range(8) for i in range(15)]
    above = send(image[TOK - W :], up_pairs)
    below = send(image[:W], [(b, a) for a, b in up_pairs])

    stats = pl.pallas_call(
        stats_kernel,
        in_specs=[SMEM, VMEM],
        out_specs=VMEM,
        out_shape=shape((2, C), F32),
        compiler_params=params(16),
    )(place, image)
    affine = combine(stats, height, opening_scale_vector, opening_offset_vector)

    a_far = send(a_up, Y_UP)
    b_up = send(a_up, X_HI)
    b_down = send(b_own, Y_DOWN)
    first = pl.pallas_call(
        activate_kernel,
        in_specs=[SMEM] + [VMEM] * 4,
        out_specs=VMEM,
        out_shape=shape((TOK + 2 * W, C), BF16),
        compiler_params=params(16),
    )(place, image, above, below, affine)

    b_far = jnp.concatenate(
        [
            send(a_far[:128], X_HI),
            send(b_up[128:256], Y_UP),
            send(b_down[256:], Y_DOWN),
        ],
        axis=0,
    )
    mine = [a_up, a_down, b_own, a_far, b_up, b_down, b_far]
    theirs = [send(block, SIBLING) for block in mine]
    x_hi, y = at_image // 4, at_image % 4
    a_at = lambda by: x_hi * 4 + (y + by) % 4
    b_at = lambda by: (1 - x_hi) * 4 + (y + by) % 4
    conv_place = jnp.stack(
        [first_row, height, core, at_image]
        + [a_at(3), a_at(1), b_at(0), a_at(2), b_at(3), b_at(1), b_at(2)]
    )
    resid, stats = pl.pallas_call(
        conv_kernel,
        in_specs=[SMEM, VMEM, VMEM, VMEM] + [ANY] * 15,
        out_specs=[VMEM, VMEM],
        out_shape=[shape((TOK, C), BF16), shape((2, C), F32)],
        scratch_shapes=[pltpu.VMEM((9, C, C), BF16), pltpu.SemaphoreType.DMA((9,))],
        compiler_params=params(40),
    )(conv_place, first, image, kernel_offset_vector[None, :], own, *mine, *theirs)
    affine = combine(stats, height, closing_scale_vector, closing_offset_vector)
    second = pl.pallas_call(
        second_kernel,
        in_specs=[SMEM, VMEM, VMEM],
        out_specs=VMEM,
        out_shape=shape((TOK, C), BF16),
        compiler_params=params(16),
    )(place, resid, affine)

    x_lo, z = at_patch // 8, at_patch // 2 % 4
    c_row = lambda by: (x_lo * 8 + (z + by) % 4 * 2 + core) * RP
    d_row = lambda by: ((1 - x_lo) * 8 + (z + by) % 4 * 2 + core) * RP
    wv_t, wq_t = value_weight.T, query_weight.T

    def project(blocks, rows):
        sizes = [block.shape[0] for block in blocks]
        count = sum(sizes)
        return pl.pallas_call(
            functools.partial(project_kernel, sizes),
            in_specs=[SMEM] + [VMEM] * (len(blocks) + 2),
            out_specs=[VMEM, VMEM],
            out_shape=[shape((count, C), BF16), shape((HEADS, VROWS, count), BF16)],
            scratch_shapes=[pltpu.VMEM((count, C), BF16)],
            compiler_params=params(32),
        )(jnp.stack([first_row, height] + rows), *blocks, key_weight, wv_t)

    def swap(pair):
        return [send(pair[0], SIBLING), send(pair[1], SIBLING)]

    acc_shape = (HEADS, VROWS, TOK)

    def attend(pair, acc):
        count = pair[0].shape[0]
        return pl.pallas_call(
            attend_kernel,
            grid=(count // TOK,),
            in_specs=[
                pl.BlockSpec((PAIRS, 2 * HEAD_DIM, 2 * TOK), lambda i: (0, 0, 0)),
                pl.BlockSpec((PAIRS, 8, 2 * TOK), lambda i: (0, 0, 0)),
                pl.BlockSpec((TOK, C), lambda i: (i, 0)),
                pl.BlockSpec((HEADS, VROWS, TOK), lambda i: (0, 0, i)),
                pl.BlockSpec(acc_shape, lambda i: (0, 0, 0)),
            ],
            out_specs=pl.BlockSpec(acc_shape, lambda i: (0, 0, 0)),
            out_shape=shape(acc_shape, F32),
            input_output_aliases={4: 0},
            compiler_params=params(40),
            cost_estimate=pl.CostEstimate(
                flops=count * TOK * C * 16, bytes_accessed=count * C * 4, transcendentals=0
            ),
        )(query, top, pair[0], pair[1], acc)

    c_up = send(second, Z_UP)
    c_down = send(second, Z_DOWN)
    d_own = send(second, X_LO)
    stage_0 = project([second], [c_row(0)])
    other_0 = swap(stage_0)
    query = pl.pallas_call(
        query_kernel,
        in_specs=[VMEM, VMEM],
        out_specs=VMEM,
        out_shape=shape((PAIRS, 2 * HEAD_DIM, 2 * TOK), BF16),
        compiler_params=params(16),
    )(second, wq_t)
    acc, top = pl.pallas_call(
        open_kernel,
        in_specs=[VMEM] * 3,
        out_specs=[VMEM] * 2,
        out_shape=[shape(acc_shape, F32), shape((PAIRS, 8, 2 * TOK), F32)],
        compiler_params=params(40),
        cost_estimate=pl.CostEstimate(
            flops=TOK * TOK * C * 16, bytes_accessed=TOK * C * 4, transcendentals=0
        ),
    )(query, *stage_0)
    acc = attend(other_0, acc)

    c_far = send(c_up, Z_UP)
    d_up = send(c_up, X_LO)
    d_down = send(d_own, Z_DOWN)
    stage_1 = project([c_up, c_down, d_own], [c_row(3), c_row(1), d_row(0)])
    other_1 = swap(stage_1)
    acc = attend(stage_1, acc)
    acc = attend(other_1, acc)

    d_far = [send(c_far[:176], X_LO), send(d_up[176:352], Z_UP), send(d_down[352:], Z_DOWN)]
    stage_2 = project([c_far, d_up, d_down], [c_row(2), d_row(3), d_row(1)])
    other_2 = swap(stage_2)
    acc = attend(stage_2, acc)
    acc = attend(other_2, acc)

    stage_3 = project(d_far, [d_row(2)])
    other_3 = swap(stage_3)
    acc = attend(stage_3, acc)
    acc = attend(other_3, acc)

    out, far = pl.pallas_call(
        finish_kernel,
        in_specs=[SMEM] + [VMEM] * 4,
        out_specs=[VMEM, SMEM],
        out_shape=[shape((TOK, C), BF16), shape((1, 1), jnp.int32)],
        compiler_params=params(32),
    )(place, acc, resid, out_weight, out_bias[None, :])
    stages = [stage_0, other_0, stage_1, other_1, stage_2, other_2, stage_3, other_3]
    live = ((jnp.arange(TOK, dtype=jnp.int32) // W + first_row) < height).astype(F32)[:, None]
    out = lax.cond(
        far[0, 0] > 0,
        lambda: exact_attention(
            query,
            [s[0] for s in stages],
            [s[1] for s in stages],
            resid,
            out_weight,
            out_bias,
            live,
        ),
        lambda: out,
    )
    return out.reshape(1, RP, W, C)


def solution(mesh):
    in_specs = (
        P("image", "patch", None, None),
        P("image"),
        P(),
        P(),
        P(None, None, "image", None),
        P(),
        P(),
        P(),
        P(),
        P(),
        P(),
        P(),
        P(),
    )
    out_specs = P("image", "patch", None, None)
    return jax.shard_map(
        per_device, mesh=mesh, in_specs=in_specs, out_specs=out_specs, check_vma=False
    )
```

time: 449 us -> 559 us (1.24)
  the two profiles are of different devices: /device:TPU:1 before, /device:TPU:69 now
where the time goes in v1:
time: 559 us; the launch traced here: 550 us
  matrix products  181 us (32%)
  Pallas kernels  85 us (15%)
  other arithmetic  79.6 us (14%)
  starting transfers between devices  61.1 us (11%)
  local copies, waits for them, and re-layouts  54 us (10%)
  loops' own time  44.6 us (8%)
  waiting for transfers between devices  42.6 us (8%)
    dot_general x10, matrix products, one_head(): s = jnp.dot(k, q, preferred_element_type=F32) * HEAD_DIM ** (-0.5)  92.1 us
    dot_general x10, matrix products, one_head(): jnp.dot(v, weights.astype(BF16), preferred_element_type=F32) / total  87.7 us
    reduce_sum x10, other arithmetic, one_head(): total = jnp.sum(weights, axis=0, keepdims=True)  77.7 us
    ppermute x35, starting transfers between devices, send(): return lax.ppermute(block, BOTH, pairs)  46.2 us
    another operation x1, loops' own time, exact_attention(): lax.map(one_head, jnp.arange(HEADS, dtype=jnp.int32)).reshape(C, TOK)  44.2 us
    pallas_call x7, Pallas kernels, attend(): pl.pallas_call(attend_kernel, grid=(count // TOK,), in_specs=[pl.BlockSpe...  43 us
    ppermute x35, waiting for transfers between devices, send(): return lax.ppermute(block, BOTH, pairs)  38.7 us
    cond x18, local copies, waits for them, and re-layouts  23.1 us
  transfers between devices with their start and end apart: 37, of which 10 were waited for; matrix products, arithmetic and copies ran while one was open for 3% of the time, Pallas kernels for 11%

profile of v1, /device:TPU:69, one launch (start us, length us, event | category | flops | bytes accessed | tf_op | source)
XLA Modules:
  0.0 549.9 jit_solution(9920261774519656979)
XLA Ops:
  4.9 10.2 %collective-permute-done.2.refs_0_ = bf16[368,640]{1,0:T(8,128)(2,1)S(1)} collective-permute-done((bf16[368,640]{1,0:T(8,128)(2,1)}, bf16[368,640]{1,0:T(8,128)(2,1)S(1)}, u32[]{:S(2)}, u32[]{:S(2)}) %collective-permute-start.2) | collective-permute-done | bytes 471072 | tf_op jit(solution)/shard_map/ppermute | solution.py:61
  61.1 15.0 %shard_map.131 = (bf16[512,640]{1,0:T(8,128)(2,1)}, f32[2,640]{1,0:T(2,128)S(1)}) custom-call(s32[11]{0:T(128)S(1)} %stack.106.place_ref, bf16[640,640]{1,0:T(8,128)(2,1)S(1)} %shard_map.130.first_ref, bf16[512,640]{1,0:T(8,128)(2,1)S(1)} %bitcast.64, f32[1,640]{1,0:T(1,128)S(1)} %broadcast_in_dim.47.bias_ref, bf16[720,640]{1,0:T(8,128)(2,1)S(1)} %bitcast.67, ...), custom_call_target="tpu_custom_call" | custom-call | tf_op jit(solution)/shard_map/pallas_call | solution.py:362
  95.1 12.2 %collective-permute-done.18.refs_0_ = bf16[512,640]{1,0:T(8,128)(2,1)} collective-permute-done((bf16[512,640]{1,0:T(8,128)(2,1)S(1)}, bf16[512,640]{1,0:T(8,128)(2,1)}, u32[]{:S(2)}, u32[]{:S(2)}) %collective-permute-start.18) | collective-permute-done | bytes 655392 | tf_op jit(solution)/shard_map/ppermute | solution.py:61
  120.5 11.7 %collective-permute-start.31 = (bf16[1536,640]{1,0:T(8,128)(2,1)}, bf16[1536,640]{1,0:T(8,128)(2,1)}, u32[]{:S(2)}, u32[]{:S(2)}) collective-permute-start(bf16[1536,640]{1,0:T(8,128)(2,1)} %get-tuple-element.189.keys_ref), channel_id=1, source_target_pairs={{0,1},{1,0},{2,3},{3,2},{4,5},{5,4},{6,7},{7,6},{16,17},{17,16},{1... | collective-permute-start | bytes 5898248 | tf_op jit(solution)/shard_map/ppermute | solution.py:61
  171.3 9.1 %shard_map.140.held_ref = f32[10,80,512]{2,1,0:T(8,128)S(1)} custom-call(bf16[5,128,1024]{2,1,0:T(8,128)(2,1)S(1)} %shard_map.133.query_ref, f32[5,8,1024]{2,1,0:T(8,128)S(1)} %get-tuple-element.184.top_ref, bf16[1536,640]{1,0:T(8,128)(2,1)} %get-tuple-element.189.keys_ref, ...), custom_call_target="tpu_custom_call", output_to_operand_aliasing={{}: (4, {})} | custom-call | flops 8053063680 | bytes 3932160 | tf_op jit(solution)/shard_map/pallas_call | solution.py:403
  183.0 9.1 %shard_map.141.held_ref = f32[10,80,512]{2,1,0:T(8,128)S(1)} custom-call(bf16[5,128,1024]{2,1,0:T(8,128)(2,1)S(1)} %shard_map.133.query_ref, f32[5,8,1024]{2,1,0:T(8,128)S(1)} %get-tuple-element.184.top_ref, bf16[1536,640]{1,0:T(8,128)(2,1)} %collective-permute-done.31.keys_ref, ...), custom_call_target="tpu_custom_call", output_to_operand_aliasing={{}: (4, {})} | custom-call | flops 8053063680 | bytes 3932160 | tf_op jit(solution)/shard_map/pallas_call | solution.py:403
  215.5 333.1 %conditional.1 = (bf16[1,8,64,640]{3,2,1,0:T(8,128)(2,1)S(1)}) conditional(s32[]{:T(128)} %bitcast.33, bf16[512,640]{1,0:T(8,128)(2,1)S(1)} %get-tuple-element.193, (bf16[512,640]{1,0:T(8,128)(2,1)S(1)}, bf16[512,640]{1,0:T(8,128)(2,1)}, bf16[512,640]{1,0:T(8,128)(2,1)}, bf16[1536,640]{1,0:T(8,128)(2,1)}, bf16[1536,640]{1,0:T(8,128)(2,1)}, ...), branch_computations={%region_8.9_spmd, %region_9.14_spmd} | conditional | flops 1541020672 | bytes 161316672 | solution.py:474
  240.1 307.6 %while.11 = (s32[]{:T(128)}, bf16[10,64,512]{2,1,0:T(8,128)(2,1)S(1)}, s32[10]{0:T(128)S(1)}, bf16[10,80,8192]{2,1,0:T(8,128)(2,1)}, pred[8192]{0:T(1024)(128)(4...) while((s32[]{:T(128)}, ...), condition=%wide.region_13.13_spmd, body=%wide.region_10.12_spmd.sunk | while | flops 1119943680 | bytes 53644356 | solution.py:269
  243.8 9.2 %fusion.47 = (f32[512]{0:T(512)S(1)}, f32[8192,512]{1,0:T(8,128)}) fusion(pred[8192]{0:T(1024)(128)(4,1)S(1)} %get-tuple-element.304, bf16[5,128,1024]{2,1,0:T(8,128)(2,1)} %get-tuple-element.306, s32[]{:T(128)S(6)} %select_n.193, s32[]{:T(128)S(6)} %select_n.195, s32[]{:T(128)S(6)} %select_n.196, bf16[8192,640]{1,0:T(8,128)(2,1)} %get-tuple-element.305, ...), kind=kOutput, calls=%fused_computation.2.clone.1 | convolution fusion | flops 549453312 | bytes 18950160 | tf_op jit(solution)/shard_map/cond/branch_1_fun/while/body/eval_jaxpr/dot_general | solution.py:263
  262.1 8.8 %fusion.49 = bf16[10,64,512]{2,1,0:T(8,128)(2,1)S(1)} fusion(bf16[10,64,512]{2,1,0:T(8,128)(2,1)S(1)} %get-tuple-element.283, s32[]{:T(128)} %get-tuple-element.282, f32[8192,512]{1,0:T(8,128)} %get-tuple-element.262, f32[512]{0:T(512)S(1)} %get-tuple-element.263, pred[8192]{0:T(1024)(128)(4,1)S(1)} %get-tuple-element.304, ...), kind=kOutput, calls=%fused_computation.12.clone.1 | convolution fusion | flops 553713664 | bytes 17904132 | tf_op jit(solution)/shard_map/cond/branch_1_fun/while/body/eval_jaxpr/dot_general | solution.py:267
  274.6 9.2 %fusion.47 = (f32[512]{0:T(512)S(1)}, f32[8192,512]{1,0:T(8,128)}) fusion(pred[8192]{0:T(1024)(128)(4,1)S(1)} %get-tuple-element.304, bf16[5,128,1024]{2,1,0:T(8,128)(2,1)} %get-tuple-element.306, s32[]{:T(128)S(6)} %select_n.193, s32[]{:T(128)S(6)} %select_n.195, s32[]{:T(128)S(6)} %select_n.196, bf16[8192,640]{1,0:T(8,128)(2,1)} %get-tuple-element.305, ...), kind=kOutput, calls=%fused_computation.2.clone.1 | convolution fusion | flops 549453312 | bytes 18950160 | tf_op jit(solution)/shard_map/cond/branch_1_fun/while/body/eval_jaxpr/dot_general | solution.py:263
  292.8 8.8 %fusion.49 = bf16[10,64,512]{2,1,0:T(8,128)(2,1)S(1)} fusion(bf16[10,64,512]{2,1,0:T(8,128)(2,1)S(1)} %get-tuple-element.283, s32[]{:T(128)} %get-tuple-element.282, f32[8192,512]{1,0:T(8,128)} %get-tuple-element.262, f32[512]{0:T(512)S(1)} %get-tuple-element.263, pred[8192]{0:T(1024)(128)(4,1)S(1)} %get-tuple-element.304, ...), kind=kOutput, calls=%fused_computation.12.clone.1 | convolution fusion | flops 553713664 | bytes 17904132 | tf_op jit(solution)/shard_map/cond/branch_1_fun/while/body/eval_jaxpr/dot_general | solution.py:267
  305.4 9.2 %fusion.47 = (f32[512]{0:T(512)S(1)}, f32[8192,512]{1,0:T(8,128)}) fusion(pred[8192]{0:T(1024)(128)(4,1)S(1)} %get-tuple-element.304, bf16[5,128,1024]{2,1,0:T(8,128)(2,1)} %get-tuple-element.306, s32[]{:T(128)S(6)} %select_n.193, s32[]{:T(128)S(6)} %select_n.195, s32[]{:T(128)S(6)} %select_n.196, bf16[8192,640]{1,0:T(8,128)(2,1)} %get-tuple-element.305, ...), kind=kOutput, calls=%fused_computation.2.clone.1 | convolution fusion | flops 549453312 | bytes 18950160 | tf_op jit(solution)/shard_map/cond/branch_1_fun/while/body/eval_jaxpr/dot_general | solution.py:263
  323.6 8.8 %fusion.49 = bf16[10,64,512]{2,1,0:T(8,128)(2,1)S(1)} fusion(bf16[10,64,512]{2,1,0:T(8,128)(2,1)S(1)} %get-tuple-element.283, s32[]{:T(128)} %get-tuple-element.282, f32[8192,512]{1,0:T(8,128)} %get-tuple-element.262, f32[512]{0:T(512)S(1)} %get-tuple-element.263, pred[8192]{0:T(1024)(128)(4,1)S(1)} %get-tuple-element.304, ...), kind=kOutput, calls=%fused_computation.12.clone.1 | convolution fusion | flops 553713664 | bytes 17904132 | tf_op jit(solution)/shard_map/cond/branch_1_fun/while/body/eval_jaxpr/dot_general | solution.py:267
  336.1 9.2 %fusion.47 = (f32[512]{0:T(512)S(1)}, f32[8192,512]{1,0:T(8,128)}) fusion(pred[8192]{0:T(1024)(128)(4,1)S(1)} %get-tuple-element.304, bf16[5,128,1024]{2,1,0:T(8,128)(2,1)} %get-tuple-element.306, s32[]{:T(128)S(6)} %select_n.193, s32[]{:T(128)S(6)} %select_n.195, s32[]{:T(128)S(6)} %select_n.196, bf16[8192,640]{1,0:T(8,128)(2,1)} %get-tuple-element.305, ...), kind=kOutput, calls=%fused_computation.2.clone.1 | convolution fusion | flops 549453312 | bytes 18950160 | tf_op jit(solution)/shard_map/cond/branch_1_fun/while/body/eval_jaxpr/dot_general | solution.py:263
  366.9 9.2 %fusion.47 = (f32[512]{0:T(512)S(1)}, f32[8192,512]{1,0:T(8,128)}) fusion(pred[8192]{0:T(1024)(128)(4,1)S(1)} %get-tuple-element.304, bf16[5,128,1024]{2,1,0:T(8,128)(2,1)} %get-tuple-element.306, s32[]{:T(128)S(6)} %select_n.193, s32[]{:T(128)S(6)} %select_n.195, s32[]{:T(128)S(6)} %select_n.196, bf16[8192,640]{1,0:T(8,128)(2,1)} %get-tuple-element.305, ...), kind=kOutput, calls=%fused_computation.2.clone.1 | convolution fusion | flops 549453312 | bytes 18950160 | tf_op jit(solution)/shard_map/cond/branch_1_fun/while/body/eval_jaxpr/dot_general | solution.py:263
  385.1 8.8 %fusion.49 = bf16[10,64,512]{2,1,0:T(8,128)(2,1)S(1)} fusion(bf16[10,64,512]{2,1,0:T(8,128)(2,1)S(1)} %get-tuple-element.283, s32[]{:T(128)} %get-tuple-element.282, f32[8192,512]{1,0:T(8,128)} %get-tuple-element.262, f32[512]{0:T(512)S(1)} %get-tuple-element.263, pred[8192]{0:T(1024)(128)(4,1)S(1)} %get-tuple-element.304, ...), kind=kOutput, calls=%fused_computation.12.clone.1 | convolution fusion | flops 553713664 | bytes 17904132 | tf_op jit(solution)/shard_map/cond/branch_1_fun/while/body/eval_jaxpr/dot_general | solution.py:267
  397.7 9.2 %fusion.47 = (f32[512]{0:T(512)S(1)}, f32[8192,512]{1,0:T(8,128)}) fusion(pred[8192]{0:T(1024)(128)(4,1)S(1)} %get-tuple-element.304, bf16[5,128,1024]{2,1,0:T(8,128)(2,1)} %get-tuple-element.306, s32[]{:T(128)S(6)} %select_n.193, s32[]{:T(128)S(6)} %select_n.195, s32[]{:T(128)S(6)} %select_n.196, bf16[8192,640]{1,0:T(8,128)(2,1)} %get-tuple-element.305, ...), kind=kOutput, calls=%fused_computation.2.clone.1 | convolution fusion | flops 549453312 | bytes 18950160 | tf_op jit(solution)/shard_map/cond/branch_1_fun/while/body/eval_jaxpr/dot_general | solution.py:263
  428.4 9.2 %fusion.47 = (f32[512]{0:T(512)S(1)}, f32[8192,512]{1,0:T(8,128)}) fusion(pred[8192]{0:T(1024)(128)(4,1)S(1)} %get-tuple-element.304, bf16[5,128,1024]{2,1,0:T(8,128)(2,1)} %get-tuple-element.306, s32[]{:T(128)S(6)} %select_n.193, s32[]{:T(128)S(6)} %select_n.195, s32[]{:T(128)S(6)} %select_n.196, bf16[8192,640]{1,0:T(8,128)(2,1)} %get-tuple-element.305, ...), kind=kOutput, calls=%fused_computation.2.clone.1 | convolution fusion | flops 549453312 | bytes 18950160 | tf_op jit(solution)/shard_map/cond/branch_1_fun/while/body/eval_jaxpr/dot_general | solution.py:263
  446.7 8.8 %fusion.49 = bf16[10,64,512]{2,1,0:T(8,128)(2,1)S(1)} fusion(bf16[10,64,512]{2,1,0:T(8,128)(2,1)S(1)} %get-tuple-element.283, s32[]{:T(128)} %get-tuple-element.282, f32[8192,512]{1,0:T(8,128)} %get-tuple-element.262, f32[512]{0:T(512)S(1)} %get-tuple-element.263, pred[8192]{0:T(1024)(128)(4,1)S(1)} %get-tuple-element.304, ...), kind=kOutput, calls=%fused_computation.12.clone.1 | convolution fusion | flops 553713664 | bytes 17904132 | tf_op jit(solution)/shard_map/cond/branch_1_fun/while/body/eval_jaxpr/dot_general | solution.py:267
  459.2 9.2 %fusion.47 = (f32[512]{0:T(512)S(1)}, f32[8192,512]{1,0:T(8,128)}) fusion(pred[8192]{0:T(1024)(128)(4,1)S(1)} %get-tuple-element.304, bf16[5,128,1024]{2,1,0:T(8,128)(2,1)} %get-tuple-element.306, s32[]{:T(128)S(6)} %select_n.193, s32[]{:T(128)S(6)} %select_n.195, s32[]{:T(128)S(6)} %select_n.196, bf16[8192,640]{1,0:T(8,128)(2,1)} %get-tuple-element.305, ...), kind=kOutput, calls=%fused_computation.2.clone.1 | convolution fusion | flops 549453312 | bytes 18950160 | tf_op jit(solution)/shard_map/cond/branch_1_fun/while/body/eval_jaxpr/dot_general | solution.py:263
  490.0 9.2 %fusion.47 = (f32[512]{0:T(512)S(1)}, f32[8192,512]{1,0:T(8,128)}) fusion(pred[8192]{0:T(1024)(128)(4,1)S(1)} %get-tuple-element.304, bf16[5,128,1024]{2,1,0:T(8,128)(2,1)} %get-tuple-element.306, s32[]{:T(128)S(6)} %select_n.193, s32[]{:T(128)S(6)} %select_n.195, s32[]{:T(128)S(6)} %select_n.196, bf16[8192,640]{1,0:T(8,128)(2,1)} %get-tuple-element.305, ...), kind=kOutput, calls=%fused_computation.2.clone.1 | convolution fusion | flops 549453312 | bytes 18950160 | tf_op jit(solution)/shard_map/cond/branch_1_fun/while/body/eval_jaxpr/dot_general | solution.py:263
  508.2 8.8 %fusion.49 = bf16[10,64,512]{2,1,0:T(8,128)(2,1)S(1)} fusion(bf16[10,64,512]{2,1,0:T(8,128)(2,1)S(1)} %get-tuple-element.283, s32[]{:T(128)} %get-tuple-element.282, f32[8192,512]{1,0:T(8,128)} %get-tuple-element.262, f32[512]{0:T(512)S(1)} %get-tuple-element.263, pred[8192]{0:T(1024)(128)(4,1)S(1)} %get-tuple-element.304, ...), kind=kOutput, calls=%fused_computation.12.clone.1 | convolution fusion | flops 553713664 | bytes 17904132 | tf_op jit(solution)/shard_map/cond/branch_1_fun/while/body/eval_jaxpr/dot_general | solution.py:267
  520.7 9.2 %fusion.47 = (f32[512]{0:T(512)S(1)}, f32[8192,512]{1,0:T(8,128)}) fusion(pred[8192]{0:T(1024)(128)(4,1)S(1)} %get-tuple-element.304, bf16[5,128,1024]{2,1,0:T(8,128)(2,1)} %get-tuple-element.306, s32[]{:T(128)S(6)} %select_n.193, s32[]{:T(128)S(6)} %select_n.195, s32[]{:T(128)S(6)} %select_n.196, bf16[8192,640]{1,0:T(8,128)(2,1)} %get-tuple-element.305, ...), kind=kOutput, calls=%fused_computation.2.clone.1 | convolution fusion | flops 549453312 | bytes 18950160 | tf_op jit(solution)/shard_map/cond/branch_1_fun/while/body/eval_jaxpr/dot_general | solution.py:263
  (227 shorter events, 290.9 us)
Async XLA Ops:
  1.9 13.2 %collective-permute-start.2 = (bf16[368,640]{1,0:T(8,128)(2,1)}, bf16[368,640]{1,0:T(8,128)(2,1)S(1)}, u32[]{:S(2)}, u32[]{:S(2)}) collective-permute-start(bf16[368,640]{1,0:T(8,128)(2,1)} %constant_dynamic-slice_fusion), channel_id=1, source_target_pairs={{0,16},{1,17},{2,18},{3,19},{4,20},{5,21},{6,22},{7,23},{16,32},{1... | collective-permute-start | bytes 1413128 | tf_op jit(solution)/shard_map/ppermute | solution.py:61
  3.2 23.1 %collective-permute-start.4 = (bf16[368,640]{1,0:T(8,128)(2,1)}, bf16[368,640]{1,0:T(8,128)(2,1)S(1)}, u32[]{:S(2)}, u32[]{:S(2)}) collective-permute-start(bf16[368,640]{1,0:T(8,128)(2,1)} %constant_dynamic-slice_fusion), channel_id=1, source_target_pairs={{0,72},{1,73},{2,74},{3,75},{4,76},{5,77},{6,78},{7,79},{16,88},{1... | collective-permute-start | bytes 1413128 | tf_op jit(solution)/shard_map/ppermute | solution.py:61
  3.5 29.6 %collective-permute-start.3 = (bf16[368,640]{1,0:T(8,128)(2,1)}, bf16[368,640]{1,0:T(8,128)(2,1)}, u32[]{:S(2)}, u32[]{:S(2)}) collective-permute-start(bf16[368,640]{1,0:T(8,128)(2,1)} %constant_dynamic-slice_fusion), channel_id=1, source_target_pairs={{0,48},{1,49},{2,50},{3,51},{4,52},{5,53},{6,54},{7,55},{16,0},{17... | collective-permute-start | bytes 1413128 | tf_op jit(solution)/shard_map/ppermute | solution.py:61
  15.1 18.0 %collective-permute-start.5 = (bf16[368,640]{1,0:T(8,128)(2,1)S(1)}, bf16[368,640]{1,0:T(8,128)(2,1)S(1)}, u32[]{:S(2)}, u32[]{:S(2)}) collective-permute-start(bf16[368,640]{1,0:T(8,128)(2,1)S(1)} %collective-permute-done.2.refs_0_), channel_id=1, source_target_pairs={{0,16},{1,17},{2,18},{3,19},{4,20},{5,21},{6,22},{7,23},{16,32},{1... | collective-permute-start | bytes 1413128 | tf_op jit(solution)/shard_map/ppermute | solution.py:61
  18.8 15.9 %all-to-all-start = ((f32[16,2,640]{2,1,0:T(2,128)}), f32[16,2,640]{2,1,0:T(2,128)S(1)}, u32[]{:S(2)}, u32[]{:S(2)}) async-start(f32[16,2,640]{2,1,0:T(2,128)} %broadcast_in_dim.40), calls=%async_computation | async-start | bytes 163840 | tf_op jit(solution)/shard_map/all_to_all | solution.py:277
  25.8 12.0 %collective-permute-start.6 = (bf16[368,640]{1,0:T(8,128)(2,1)S(1)}, bf16[368,640]{1,0:T(8,128)(2,1)S(1)}, u32[]{:S(2)}, u32[]{:S(2)}) collective-permute-start(bf16[368,640]{1,0:T(8,128)(2,1)S(1)} %collective-permute-done.2.refs_0_), channel_id=1, source_target_pairs={{0,72},{1,73},{2,74},{3,75},{4,76},{5,77},{6,78},{7,79},{16,88},{1... | collective-permute-start | bytes 1413128 | tf_op jit(solution)/shard_map/ppermute | solution.py:61
  26.4 13.8 %collective-permute-start.7 = (bf16[368,640]{1,0:T(8,128)(2,1)S(1)}, bf16[368,640]{1,0:T(8,128)(2,1)S(1)}, u32[]{:S(2)}, u32[]{:S(2)}) collective-permute-start(bf16[368,640]{1,0:T(8,128)(2,1)S(1)} %collective-permute-done.4.refs_2_), channel_id=1, source_target_pairs={{0,48},{1,49},{2,50},{3,51},{4,52},{5,53},{6,54},{7,55},{16,0},{17... | collective-permute-start | bytes 1413128 | tf_op jit(solution)/shard_map/ppermute | solution.py:61
  32.1 21.2 %collective-permute-start.11 = (bf16[368,640]{1,0:T(8,128)(2,1)S(1)}, bf16[368,640]{1,0:T(8,128)(2,1)}, u32[]{:S(2)}, u32[]{:S(2)}) collective-permute-start(bf16[368,640]{1,0:T(8,128)(2,1)S(1)} %collective-permute-done.2.refs_0_), channel_id=1, source_target_pairs={{0,1},{1,0},{2,3},{3,2},{4,5},{5,4},{6,7},{7,6},{16,17},{17,16},{1... | collective-permute-start | bytes 1413128 | tf_op jit(solution)/shard_map/ppermute | solution.py:61
  33.1 20.7 %collective-permute-start.12 = (bf16[368,640]{1,0:T(8,128)(2,1)}, bf16[368,640]{1,0:T(8,128)(2,1)}, u32[]{:S(2)}, u32[]{:S(2)}) collective-permute-start(bf16[368,640]{1,0:T(8,128)(2,1)} %collective-permute-done.3.refs_1_), channel_id=1, source_target_pairs={{0,1},{1,0},{2,3},{3,2},{4,5},{5,4},{6,7},{7,6},{16,17},{17,16},{1... | collective-permute-start | bytes 1413128 | tf_op jit(solution)/shard_map/ppermute | solution.py:61
  76.8 11.8 %all-to-all-start.1 = ((f32[16,2,640]{2,1,0:T(2,128)}), f32[16,2,640]{2,1,0:T(2,128)S(1)}, u32[]{:S(2)}, u32[]{:S(2)}) async-start(f32[16,2,640]{2,1,0:T(2,128)} %broadcast_in_dim.80), calls=%async_computation.1 | async-start | bytes 163840 | tf_op jit(solution)/shard_map/all_to_all | solution.py:277
  91.3 16.1 %collective-permute-start.18 = (bf16[512,640]{1,0:T(8,128)(2,1)S(1)}, bf16[512,640]{1,0:T(8,128)(2,1)}, u32[]{:S(2)}, u32[]{:S(2)}) collective-permute-start(bf16[512,640]{1,0:T(8,128)(2,1)S(1)} %shard_map.132.second_ref.refs_0_), channel_id=1, source_target_pairs={{0,2},{1,3},{2,4},{3,5},{4,6},{5,7},{6,0},{7,1},{16,18},{17,19},{1... | collective-permute-start | bytes 1966088 | tf_op jit(solution)/shard_map/ppermute | solution.py:61
  92.6 15.7 %collective-permute-start.23 = (bf16[512,640]{1,0:T(8,128)(2,1)S(1)}, bf16[512,640]{1,0:T(8,128)(2,1)S(1)}, u32[]{:S(2)}, u32[]{:S(2)}) collective-permute-start(bf16[512,640]{1,0:T(8,128)(2,1)S(1)} %shard_map.132.second_ref.refs_0_), channel_id=1, source_target_pairs={{0,8},{1,9},{2,10},{3,11},{4,12},{5,13},{6,14},{7,15},{16,24},{17,... | collective-permute-start | bytes 1966088 | tf_op jit(solution)/shard_map/ppermute | solution.py:61
  92.9 15.9 %collective-permute-start.30 = (bf16[512,640]{1,0:T(8,128)(2,1)S(1)}, bf16[512,640]{1,0:T(8,128)(2,1)}, u32[]{:S(2)}, u32[]{:S(2)}) collective-permute-start(bf16[512,640]{1,0:T(8,128)(2,1)S(1)} %shard_map.132.second_ref.refs_0_), channel_id=1, source_target_pairs={{0,6},{1,7},{2,0},{3,1},{4,2},{5,3},{6,4},{7,5},{16,22},{17,23},{1... | collective-permute-start | bytes 1966088 | tf_op jit(solution)/shard_map/ppermute | solution.py:61
  115.1 67.9 %collective-permute-start.32 = (bf16[10,80,1536]{2,1,0:T(8,128)(2,1)}, bf16[10,80,1536]{2,1,0:T(8,128)(2,1)}, u32[]{:S(2)}, u32[]{:S(2)}) collective-permute-start(bf16[10,80,1536]{2,1,0:T(8,128)(2,1)} %get-tuple-element.190.values_ref), channel_id=1, source_target_pairs={{0,1},{1,0},{2,3},{3,2},{4,5},{5,4},{6,7},{7,6},{16,17},{17,16},{1... | collective-permute-start | bytes 7372808 | tf_op jit(solution)/shard_map/ppermute | solution.py:61
  116.7 18.3 %collective-permute-start.19 = (bf16[512,640]{1,0:T(8,128)(2,1)}, bf16[512,640]{1,0:T(8,128)(2,1)}, u32[]{:S(2)}, u32[]{:S(2)}) collective-permute-start(bf16[512,640]{1,0:T(8,128)(2,1)} %collective-permute-done.18.refs_0_), channel_id=1, source_target_pairs={{0,2},{1,3},{2,4},{3,5},{4,6},{5,7},{6,0},{7,1},{16,18},{17,19},{1... | collective-permute-start | bytes 1966088 | tf_op jit(solution)/shard_map/ppermute | solution.py:61
  119.4 16.2 %collective-permute-start.21 = (bf16[512,640]{1,0:T(8,128)(2,1)}, bf16[512,640]{1,0:T(8,128)(2,1)S(1)}, u32[]{:S(2)}, u32[]{:S(2)}) collective-permute-start(bf16[512,640]{1,0:T(8,128)(2,1)} %collective-permute-done.18.refs_0_), channel_id=1, source_target_pairs={{0,8},{1,9},{2,10},{3,11},{4,12},{5,13},{6,14},{7,15},{16,24},{17,... | collective-permute-start | bytes 1966088 | tf_op jit(solution)/shard_map/ppermute | solution.py:61
  120.5 62.1 %collective-permute-start.31 = (bf16[1536,640]{1,0:T(8,128)(2,1)}, bf16[1536,640]{1,0:T(8,128)(2,1)}, u32[]{:S(2)}, u32[]{:S(2)}) collective-permute-start(bf16[1536,640]{1,0:T(8,128)(2,1)} %get-tuple-element.189.keys_ref), channel_id=1, source_target_pairs={{0,1},{1,0},{2,3},{3,2},{4,5},{5,4},{6,7},{7,6},{16,17},{17,16},{1... | collective-permute-start | bytes 5898248 | tf_op jit(solution)/shard_map/ppermute | solution.py:61
  135.0 24.9 %collective-permute-start.34 = (bf16[10,80,512]{2,1,0:T(8,128)(2,1)}, bf16[10,80,512]{2,1,0:T(8,128)(2,1)}, u32[]{:S(2)}, u32[]{:S(2)}) collective-permute-start(bf16[10,80,512]{2,1,0:T(8,128)(2,1)} %get-tuple-element.183.values_ref), channel_id=1, source_target_pairs={{0,1},{1,0},{2,3},{3,2},{4,5},{5,4},{6,7},{7,6},{16,17},{17,16},{1... | collective-permute-start | bytes 2457608 | tf_op jit(solution)/shard_map/ppermute | solution.py:61
  135.0 16.1 %collective-permute-start.24 = (bf16[512,640]{1,0:T(8,128)(2,1)}, bf16[512,640]{1,0:T(8,128)(2,1)}, u32[]{:S(2)}, u32[]{:S(2)}) collective-permute-start(bf16[512,640]{1,0:T(8,128)(2,1)} %copy-done.7), channel_id=1, source_target_pairs={{0,6},{1,7},{2,0},{3,1},{4,2},{5,3},{6,4},{7,5},{16,22},{17,23},{1... | collective-permute-start | bytes 1966088 | tf_op jit(solution)/shard_map/ppermute | solution.py:61
  136.4 22.8 %collective-permute-start.33 = (bf16[512,640]{1,0:T(8,128)(2,1)}, bf16[512,640]{1,0:T(8,128)(2,1)}, u32[]{:S(2)}, u32[]{:S(2)}) collective-permute-start(bf16[512,640]{1,0:T(8,128)(2,1)} %get-tuple-element.182.keys_ref), channel_id=1, source_target_pairs={{0,1},{1,0},{2,3},{3,2},{4,5},{5,4},{6,7},{7,6},{16,17},{17,16},{1... | collective-permute-start | bytes 1966088 | tf_op jit(solution)/shard_map/ppermute | solution.py:61
  155.9 44.1 %collective-permute-start.29 = (bf16[10,80,1536]{2,1,0:T(8,128)(2,1)S(1)}, bf16[10,80,1536]{2,1,0:T(8,128)(2,1)S(1)}, u32[]{:S(2)}, u32[]{:S(2)}) collective-permute-start(bf16[10,80,1536]{2,1,0:T(8,128)(2,1)S(1)} %get-tuple-element.188.values_ref), channel_id=1, source_target_pairs={{0,1},{1,0},{2,3},{3,2},{4,5},{5,4},{6,7},{7,6},{16,17},{17,16},{1... | collective-permute-start | bytes 7372808 | tf_op jit(solution)/shard_map/ppermute | solution.py:61
  167.8 32.1 %collective-permute-start.28 = (bf16[1536,640]{1,0:T(8,128)(2,1)S(1)}, bf16[1536,640]{1,0:T(8,128)(2,1)S(1)}, u32[]{:S(2)}, u32[]{:S(2)}) collective-permute-start(bf16[1536,640]{1,0:T(8,128)(2,1)S(1)} %get-tuple-element.187.keys_ref), channel_id=1, source_target_pairs={{0,1},{1,0},{2,3},{3,2},{4,5},{5,4},{6,7},{7,6},{16,17},{17,16},{1... | collective-permute-start | bytes 5898248 | tf_op jit(solution)/shard_map/ppermute | solution.py:61
  182.2 28.3 %collective-permute-start.27 = (bf16[10,80,512]{2,1,0:T(8,128)(2,1)S(1)}, bf16[10,80,512]{2,1,0:T(8,128)(2,1)S(1)}, u32[]{:S(2)}, u32[]{:S(2)}) collective-permute-start(bf16[10,80,512]{2,1,0:T(8,128)(2,1)S(1)} %get-tuple-element.186.values_ref), channel_id=1, source_target_pairs={{0,1},{1,0},{2,3},{3,2},{4,5},{5,4},{6,7},{7,6},{16,17},{17,16},{1... | collective-permute-start | bytes 2457608 | tf_op jit(solution)/shard_map/ppermute | solution.py:61
  182.5 27.9 %collective-permute-start.26 = (bf16[512,640]{1,0:T(8,128)(2,1)S(1)}, bf16[512,640]{1,0:T(8,128)(2,1)S(1)}, u32[]{:S(2)}, u32[]{:S(2)}) collective-permute-start(bf16[512,640]{1,0:T(8,128)(2,1)S(1)} %get-tuple-element.185.keys_ref), channel_id=1, source_target_pairs={{0,1},{1,0},{2,3},{3,2},{4,5},{5,4},{6,7},{7,6},{16,17},{17,16},{1... | collective-permute-start | bytes 1966088 | tf_op jit(solution)/shard_map/ppermute | solution.py:61
  (31 other events, 544.2 us)

commit v2 on v0

v2 whole, which is shorter than its diff:
```python
import functools

import jax
import jax.numpy as jnp
from jax import lax
from jax.experimental import pallas as pl
from jax.experimental.pallas import tpu as pltpu
from jax.sharding import PartitionSpec as P

HEAD_DIM = 64
GROUPS = 32
C = 640
W = 64
RP = 8
TOK = RP * W
HEADS = C // HEAD_DIM
VROWS = 80
MINE = HEADS // 2
HALF_C = C // 2
QUERIES = 2 * TOK
HALF = 368
BOTH = ("image", "patch")
SCORE_SCALE = HEAD_DIM**-0.5 * 1.4426950408889634
VMEM = pl.BlockSpec(memory_space=pltpu.VMEM)
SMEM = pl.BlockSpec(memory_space=pltpu.SMEM)
ANY = pl.BlockSpec(memory_space=pl.ANY)
HBM = pl.BlockSpec(memory_space=pltpu.HBM)
F32 = jnp.float32
BF16 = jnp.bfloat16


def params(mib):
    return pltpu.CompilerParams(vmem_limit_bytes=mib << 20)


def cost(microseconds):
    return pl.CostEstimate(
        flops=int(microseconds * 1e9), bytes_accessed=int(microseconds * 3e6), transcendentals=0
    )


def near(dims, kind):
    return pltpu.VMEM(dims, kind)


def shape(dims, kind):
    return jax.ShapeDtypeStruct(dims, kind)


def pairs_of(move):
    pairs = []
    for x in range(4):
        for y in range(4):
            for z in range(4):
                for core in range(2):
                    ends = []
                    for a, b, c, d in ((x, y, z, core), move(x, y, z, core)):
                        a, b, c = a % 4, b % 4, c % 4
                        ends.append((a // 2 * 4 + b) * 16 + a % 2 * 8 + c * 2 + d)
                    pairs.append(tuple(ends))
    return pairs


SIBLING = pairs_of(lambda x, y, z, core: (x, y, z, 1 - core))
SIBLINGS = [SIBLING, SIBLING[1:] + SIBLING[:1], SIBLING[2:] + SIBLING[:2]]
Y_UP = pairs_of(lambda x, y, z, core: (x, y + 1, z, core))
Y_DOWN = pairs_of(lambda x, y, z, core: (x, y - 1, z, core))
Z_UP = pairs_of(lambda x, y, z, core: (x, y, z + 1, core))
Z_DOWN = pairs_of(lambda x, y, z, core: (x, y, z - 1, core))
X_LO = pairs_of(lambda x, y, z, core: (x ^ 1, y, z, core))
X_HI = pairs_of(lambda x, y, z, core: (3 - x, y, z, core))


def send(block, pairs):
    return lax.ppermute(block, BOTH, pairs)


def row_live(count, first_row, height):
    rows = lax.broadcasted_iota(jnp.int32, (count, 1), 0) // W + first_row
    return jnp.where(jnp.logical_and(rows >= 0, rows < height), 1.0, 0.0)


def spread(stats_ref, cells, live, live_count):
    mean = jnp.sum(cells * live, axis=0, keepdims=True) / jnp.maximum(live_count, 1.0)
    centred = (cells - mean) * live
    both = jnp.concatenate([mean, jnp.sum(centred * centred, axis=0, keepdims=True)], axis=0)
    for i in range(16):
        stats_ref[i] = both


def stats_kernel(place_ref, image_ref, out_ref):
    first_row, height = place_ref[0], place_ref[1]
    count = (jnp.clip(height - first_row, 0, RP) * W).astype(F32)
    spread(out_ref, image_ref[...].astype(F32), row_live(TOK, first_row, height), count)


def half_kernel(place_ref, own_ref, out_ref, sem):
    start = pl.multiple_of(place_ref[2] * (9 * 80 - HALF), 16)
    copy = pltpu.make_async_copy(own_ref.at[pl.ds(start, HALF), :], out_ref, sem)
    copy.start()
    copy.wait()


GROUPS_OF_SLOTS = ((0, 4, 384), (4, 3, 256), (7, 1, 128))


def activate_kernel(
    place_ref, image_ref, above_ref, below_ref, affine_ref, *outs
):
    first_row, height = place_ref[0], place_ref[1]
    mean, gain, shift = affine_ref[0:1, :], affine_ref[1:2, :], affine_ref[2:3, :]
    channel = lax.broadcasted_iota(jnp.int32, (C, 128), 0)
    order = []
    for first_slot, slots, width in GROUPS_OF_SLOTS:
        wanted = []
        for at in range(0, width, 128):
            lane = lax.broadcasted_iota(jnp.int32, (1, 128), 1) + at
            source = jnp.full((1, 128), -1, jnp.int32)
            for s in range(slots):
                base = place_ref[3 + first_slot + s] * 80 - s * 80
                inside = jnp.logical_and(lane >= s * 80, lane < (s + 1) * 80)
                source = jnp.where(inside, lane + base, source)
            wanted.append(jnp.where(channel == source, 1.0, 0.0).astype(BF16))
        order.append(jnp.concatenate(wanted, axis=1))

    def put(at, count, block, row):
        live = row_live(count, row, height)
        v = (block.astype(F32) * live - mean) * gain + shift
        active = (v / (1.0 + jnp.exp(-v)) * live).astype(BF16)
        for matrix, out in zip(order, outs):
            out[at : at + count, :] = jnp.dot(
                active, matrix, preferred_element_type=F32
            ).astype(BF16)

    put(0, W, above_ref[...], first_row - 1)
    put(W, TOK, image_ref[...], first_row)
    put(W + TOK, W, below_ref[...], first_row + RP)


def weights_kernel(place_ref, wq_ref, wk_ref, wv_ref, wq_t_ref, wk_half_ref, wv_t_ref, turned):
    first_head = pl.ds(pl.multiple_of(place_ref[2] * HALF_C, HALF_C), HALF_C)
    turned[...] = wq_ref[...].T
    wq_t_ref[...] = turned[first_head, :]
    turned[...] = wv_ref[...].T
    wv_t_ref[...] = turned[first_head, :]
    turned[...] = wk_ref[...].T
    wk_half_ref[...] = turned[first_head, :].T


def conv_part(group, place_ref, first_ref, own_ref, mine, theirs, put):
    first_slot, slots, width = GROUPS_OF_SLOTS[group]
    remote = len(mine)
    pad = width - slots * 80

    def from_mine(i, row, rows):
        return mine[i][row : row + rows, :]

    def from_theirs(i, row, rows):
        return theirs[i][row : row + rows, :]

    def run(low, high):
        columns = lax.broadcasted_iota(jnp.int32, (TOK, 1), 0) % W

        def tap_weight(tap):
            pieces = [] if own_ref is None else [own_ref[80 * tap : 80 * tap + 80, :]]
            for i in range(remote):
                if tap <= 3:
                    pieces.append(low(i, 80 * tap, 80))
                elif tap >= 5:
                    pieces.append(high(i, 80 * tap - 352, 80))
                else:
                    pieces += [low(i, 320, 48), high(i, 16, 32)]
            return jnp.concatenate(pieces + [jnp.zeros((pad, C), BF16)], axis=0)

        total = None
        for dx in (0, 1, 2):
            part = None
            for dy in range(3):
                product = jnp.dot(
                    first_ref[dy * W : dy * W + TOK, :],
                    tap_weight(dy * 3 + dx),
                    preferred_element_type=F32,
                )
                part = product if part is None else part + product
            if dx == 0:
                part = jnp.where(columns == 0, 0.0, pltpu.roll(part, 1, 0))
            if dx == 2:
                part = jnp.where(columns == W - 1, 0.0, pltpu.roll(part, TOK - 1, 0))
            total = part if total is None else total + part
        put(total)

    pl.when(place_ref[2] == 0)(lambda: run(from_mine, from_theirs))
    pl.when(place_ref[2] != 0)(lambda: run(from_theirs, from_mine))


def conv_open_kernel(place_ref, first_ref, own_ref, a, b, c, d, e, f, out_ref):
    def put(total):
        out_ref[...] = total

    conv_part(0, place_ref, first_ref, own_ref, (a, b, c), (d, e, f), put)


def conv_more_kernel(place_ref, first_ref, a, b, c, d, e, f, held_ref, out_ref):
    def put(total):
        out_ref[...] = held_ref[...] + total

    conv_part(1, place_ref, first_ref, None, (a, b, c), (d, e, f), put)


def conv_close_kernel(
    place_ref, first_ref, a, theirs_ref, held_ref, image_ref, bias_ref, resid_ref, stats_ref
):
    first_row, height = place_ref[0], place_ref[1]
    live = row_live(TOK, first_row, height)

    def put(total):
        start = image_ref[...].astype(F32) * live
        conv = held_ref[...] + total
        resid_ref[...] = ((start + conv + bias_ref[...]) * live).astype(BF16)

    conv_part(2, place_ref, first_ref, None, (a,), (theirs_ref,), put)
    count = (jnp.clip(height - first_row, 0, RP) * W).astype(F32)
    spread(stats_ref, resid_ref[...].astype(F32), live, count)


def transposed(weight_t, block):
    return lax.dot_general(
        weight_t, block, (((1,), (1,)), ((), ())), preferred_element_type=F32
    ).astype(BF16)


def normalized(place_ref, affine_ref, row, block):
    mean, gain, shift = affine_ref[0:1, :], affine_ref[1:2, :], affine_ref[2:3, :]
    v = (block.astype(F32) - mean) * gain + shift
    return (v * row_live(TOK, row, place_ref[1])).astype(BF16)


def attend_block(place_ref, affine_ref, row, block, wk_ref, wv_ref, query_ref, top_of, put, mask=None):
    second = normalized(place_ref, affine_ref, row, block)
    keys = jnp.dot(second, wk_ref[...], preferred_element_type=F32).astype(BF16)
    values = transposed(wv_ref[...], second)
    tokens = lax.broadcasted_iota(jnp.int32, (VROWS - HEAD_DIM, TOK), 1)
    lines = lax.broadcasted_iota(jnp.int32, (VROWS - HEAD_DIM, TOK), 0)
    used = jnp.logical_and(lines == 0, tokens // W + row < place_ref[1])
    ones = jnp.where(used, 1.0, 0.0).astype(BF16)
    for h in range(MINE):
        pair = keys[:, h // 2 * 128 : min((h // 2 + 1) * 128, HALF_C)]
        s = jnp.dot(pair, query_ref[h, : pair.shape[1], :], preferred_element_type=F32)
        s = s * SCORE_SCALE
        if mask is not None:
            s = mask(s)
        weights = jnp.exp2(s - top_of(h, s)).astype(BF16)
        value = jnp.concatenate([values[h * HEAD_DIM : (h + 1) * HEAD_DIM], ones], axis=0)
        put(h, jnp.dot(value, weights, preferred_element_type=F32))


def open_kernel(place_ref, affine_ref, own_ref, other_ref, wq_ref, wk_ref, wv_ref, *refs):
    query_ref, acc_ref, top_ref = refs
    blocks = ((place_ref[2], own_ref), (place_ref[3], other_ref))
    for n, (row, ref) in enumerate(blocks):
        second = normalized(place_ref, affine_ref, row, ref[...])
        q = transposed(wq_ref[...], second)
        span = slice(n * TOK, (n + 1) * TOK)
        zero = jnp.zeros((HEAD_DIM, TOK), BF16)
        for h in range(MINE):
            here, there = h % 2 * HEAD_DIM, (h + 1) % 2 * HEAD_DIM
            query_ref[h, here : here + HEAD_DIM, span] = q[h * HEAD_DIM : (h + 1) * HEAD_DIM]
            query_ref[h, there : there + HEAD_DIM, span] = zero

    def top_of(h, s):
        top = jnp.max(s, axis=0, keepdims=True)
        top_ref[h] = jnp.broadcast_to(top, (8, QUERIES))
        return top

    def put(h, update):
        acc_ref[h] = update

    def add(h, update):
        acc_ref[h] += update

    for (row, ref), tops, store in zip(
        blocks, (top_of, lambda h, s: top_ref[h, 0:1, :]), (put, add)
    ):
        attend_block(
            place_ref, affine_ref, row, ref[...], wk_ref, wv_ref, query_ref, tops, store
        )


def attend_kernel(count, place_ref, affine_ref, query_ref, top_ref, wk_ref, wv_ref, *refs):
    sources, held_ref, acc_ref, blocks, sems = refs[:count], *refs[count:]
    for n, source in enumerate(sources):
        pltpu.make_async_copy(source, blocks.at[n], sems.at[n]).start()

    def put(h, update):
        acc_ref[h] += update

    def step(n, _):
        pltpu.make_async_copy(blocks.at[n], blocks.at[n], sems.at[n]).wait()
        attend_block(
            place_ref,
            affine_ref,
            place_ref[2 + n],
            blocks[n],
            wk_ref,
            wv_ref,
            query_ref,
            lambda h, s: top_ref[h, 0:1, :],
            put,
        )
        return 0

    acc_ref[...] = held_ref[...]
    lax.fori_loop(0, count, step, 0)


def close_kernel(
    place_ref, affine_ref, query_ref, top_ref, wk_ref, wv_ref, block_ref, held_ref, *refs
):
    blocks = refs[:16]
    mixed_ref, others_ref, acc_ref, highest, block, sem = refs[16:]

    def put(h, update):
        acc_ref[h] = held_ref[h] + update

    attend_block(
        place_ref,
        affine_ref,
        place_ref[2 + 15],
        block_ref[...],
        wk_ref,
        wv_ref,
        query_ref,
        lambda h, s: top_ref[h, 0:1, :],
        put,
    )
    far = jnp.zeros((1, QUERIES), F32)
    for h in range(MINE):
        total = acc_ref[h, HEAD_DIM : HEAD_DIM + 1, :]
        inside = jnp.logical_and(total > 2.0**-60, total < 2.0**100)
        far = jnp.maximum(far, jnp.where(inside, 0.0, 1.0))

    @pl.when(jnp.max(far) > 0.0)
    def _():
        highest[...] = jnp.full(highest.shape, -1e30, F32)
        acc_ref[...] = jnp.zeros(acc_ref.shape, F32)

        def step(n, _):
            for i, source in enumerate(blocks):

                @pl.when(n == i)
                def _():
                    copy = pltpu.make_async_copy(source, block, sem)
                    copy.start()
                    copy.wait()

            row = place_ref[2 + n]
            key_live = row_live(TOK, row, place_ref[1])

            def top_of(h, s):
                before = highest[h]
                after = jnp.maximum(before, jnp.max(s, axis=0, keepdims=True))
                highest[h] = after
                acc_ref[h] = acc_ref[h] * jnp.exp2(before - after)
                return after

            def add(h, update):
                acc_ref[h] += update

            def masked(s):
                return jnp.where(key_live > 0.0, s, -1e30)

            attend_block(
                place_ref,
                affine_ref,
                row,
                block[...],
                wk_ref,
                wv_ref,
                query_ref,
                top_of,
                add,
                masked,
            )
            return 0

        lax.fori_loop(0, 16, step, 0)

    for h in range(MINE):
        total = acc_ref[h, HEAD_DIM : HEAD_DIM + 1, :]
        total = jnp.where(total > 0.0, total, 1.0)
        mixed = (acc_ref[h, 0:HEAD_DIM, :] / total).astype(BF16)
        for n, ref in enumerate((mixed_ref, others_ref)):
            ref[h * HEAD_DIM : (h + 1) * HEAD_DIM, :] = mixed[:, n * TOK : (n + 1) * TOK]


def finish_kernel(place_ref, mixed_ref, other_ref, resid_ref, wo_ref, bias_ref, out_ref):
    core = place_ref[2]
    update = None
    for at, ref in ((core, mixed_ref), (1 - core, other_ref)):
        rows = pl.ds(pl.multiple_of(at * HALF_C, HALF_C), HALF_C)
        part = lax.dot_general(
            ref[...], wo_ref[rows, :], (((0,), (0,)), ((), ())), preferred_element_type=F32
        )
        update = part if update is None else update + part
    live = row_live(TOK, place_ref[0], place_ref[1])
    out_ref[...] = ((resid_ref[...].astype(F32) + update + bias_ref[...]) * live).astype(BF16)


def exchange(stats):
    return lax.all_to_all(stats, "patch", 0, 0, tiled=False)


def combine(everyone, height, gain, shift):
    rows = jnp.clip(height - RP * jnp.arange(16, dtype=jnp.int32), 0, RP)
    counts = (rows * W).astype(F32)[:, None, None]
    entries = (height * W * (C // GROUPS)).astype(F32)
    means = everyone[:, 0].reshape(16, GROUPS, C // GROUPS)
    squares = everyone[:, 1].reshape(16, GROUPS, C // GROUPS)
    mean = jnp.sum(means * counts, axis=(0, 2)) / entries
    apart = means - mean[None, :, None]
    spread = jnp.sum(squares + counts * apart * apart, axis=(0, 2)) / entries
    scale = lax.rsqrt(spread + 1e-05)
    wide = lambda v: jnp.broadcast_to(v[:, None], (GROUPS, C // GROUPS)).reshape(C)
    return jnp.stack([wide(mean), wide(scale) * gain, shift])


def per_device(
    images,
    heights,
    opening_scale_vector,
    opening_offset_vector,
    conv_weight,
    kernel_offset_vector,
    closing_scale_vector,
    closing_offset_vector,
    query_weight,
    key_weight,
    value_weight,
    out_weight,
    out_bias,
):
    image = images[0].reshape(TOK, C)
    height = heights[0]
    at_image = lax.axis_index("image")
    at_patch = lax.axis_index("patch")
    core = at_patch % 2
    first_row = at_patch * RP
    x_hi, y = at_image // 4, at_image % 4
    x_lo, z = at_patch // 8, at_patch // 2 % 4
    a_at = lambda by: x_hi * 4 + (y + by) % 4
    b_at = lambda by: (1 - x_hi) * 4 + (y + by) % 4
    place = jnp.stack(
        [first_row, height, core, at_image]
        + [a_at(3), a_at(1), b_at(0), a_at(2), b_at(3), b_at(1), b_at(2)]
    )

    own = conv_weight.reshape(9 * 80, C)
    half = pl.pallas_call(
        half_kernel,
        in_specs=[SMEM, HBM],
        out_specs=VMEM,
        out_shape=near((HALF, C), BF16),
        scratch_shapes=[pltpu.SemaphoreType.DMA],
        compiler_params=params(8),
    )(place, own)
    a_up = send(half, Y_UP)
    a_down = send(half, Y_DOWN)
    b_own = send(half, X_HI)

    stats = pl.pallas_call(
        stats_kernel,
        in_specs=[SMEM, VMEM],
        out_specs=VMEM,
        out_shape=shape((16, 2, C), F32),
        compiler_params=params(16),
    )(place, image)
    everyone = exchange(stats)
    a_up, a_down, b_own, bottom, top_row = lax.optimization_barrier(
        (a_up, a_down, b_own, image[TOK - W :], image[:W])
    )
    a_far = send(a_up, Y_UP)
    b_up = send(a_up, X_HI)
    b_down = send(b_own, Y_DOWN)
    up_pairs = [(g * 16 + i, g * 16 + i + 1) for g in range(8) for i in range(15)]
    above = send(bottom, up_pairs)
    below = send(top_row, [(b, a) for a, b in up_pairs])
    affine = combine(everyone, height, opening_scale_vector, opening_offset_vector)

    widths = [width for _, _, width in GROUPS_OF_SLOTS]
    first = pl.pallas_call(
        activate_kernel,
        in_specs=[SMEM] + [VMEM] * 4,
        out_specs=[VMEM] * 3,
        out_shape=[near((TOK + 2 * W, width), BF16) for width in widths],
        compiler_params=params(20),
        cost_estimate=cost(3),
    )(place, image, above, below, affine)
    widths = [width for _, _, width in GROUPS_OF_SLOTS]
    first = pl.pallas_call(
        activate_kernel,
        in_specs=[SMEM] + [VMEM] * 4,
        out_specs=[VMEM] * 3,
        out_shape=[near((TOK + 2 * W, width), BF16) for width in widths],
        compiler_params=params(20),
        cost_estimate=cost(3),
    )(place, image, above, below, affine)
    theirs_1 = [send(b, p) for b, p in zip((a_up, a_down, b_own), SIBLINGS)]
    mine_1, first = lax.optimization_barrier(([a_up, a_down, b_own], first))
    theirs_1 = [send(b, p) for b, p in zip(mine_1, SIBLINGS)]
    mine_2, theirs_1, first = lax.optimization_barrier(([a_far, b_up, b_down], theirs_1, first))
    b_far = send(mine_2[0], X_HI)
    theirs_2 = [send(b, p) for b, p in zip(mine_2, SIBLINGS)]
    conv = pl.pallas_call(
        conv_open_kernel,
        in_specs=[SMEM] + [VMEM] * 8,
        out_specs=VMEM,
        out_shape=near((TOK, C), F32),
        compiler_params=params(20),
        cost_estimate=cost(5),
    )(place, first[0], own, a_up, a_down, b_own, *theirs_1)
    conv, *qkv = lax.optimization_barrier((conv, query_weight, key_weight, value_weight))
    wq_t, wk, wv_t = pl.pallas_call(
        weights_kernel,
        in_specs=[SMEM] + [VMEM] * 3,
        out_specs=[VMEM] * 3,
        out_shape=[near(dims, BF16) for dims in ((HALF_C, C), (C, HALF_C), (HALF_C, C))],
        scratch_shapes=[pltpu.VMEM((C, C), BF16)],
        compiler_params=params(20),
        cost_estimate=cost(3),
    )(place, *qkv)
    b_far, theirs_2, conv, wq_t, wk, wv_t = lax.optimization_barrier(
        (b_far, theirs_2, conv, wq_t, wk, wv_t)
    )
    conv = pl.pallas_call(
        conv_more_kernel,
        in_specs=[SMEM] + [VMEM] * 8,
        out_specs=VMEM,
        out_shape=near((TOK, C), F32),
        input_output_aliases={8: 0},
        compiler_params=params(20),
        cost_estimate=cost(4),
    )(place, first[1], *mine_2, *theirs_2, conv)
    theirs_3 = send(b_far, SIBLING)
    resid, stats = pl.pallas_call(
        conv_close_kernel,
        in_specs=[SMEM] + [VMEM] * 6,
        out_specs=[VMEM, VMEM],
        out_shape=[near((TOK, C), BF16), shape((16, 2, C), F32)],
        compiler_params=params(20),
    )(place, first[2], b_far, theirs_3, conv, image, kernel_offset_vector[None, :])

    c_up = send(resid, Z_UP)
    c_down = send(resid, Z_DOWN)
    d_own = send(resid, X_LO)
    other_0 = send(resid, SIBLING)
    everyone = exchange(stats)
    c_up, c_down, d_own, other_0, everyone = lax.optimization_barrier(
        (c_up, c_down, d_own, other_0, everyone)
    )
    affine = combine(everyone, height, closing_scale_vector, closing_offset_vector)
    c_row = lambda by, at: (x_lo * 8 + (z + by) % 4 * 2 + at) * RP
    d_row = lambda by, at: ((1 - x_lo) * 8 + (z + by) % 4 * 2 + at) * RP
    rows_of = lambda at: [
        [c_row(0, at)],
        [c_row(3, at), c_row(1, at), d_row(0, at)],
        [c_row(2, at), d_row(3, at), d_row(1, at)],
        [d_row(2, at)],
    ]
    mine, theirs = rows_of(core), rows_of(1 - core)

    def rows_place(rows):
        return jnp.stack([first_row, height] + rows)

    acc_shape = (MINE, VROWS, QUERIES)

    def attend(blocks, rows, acc):
        return pl.pallas_call(
            functools.partial(attend_kernel, len(blocks)),
            in_specs=[SMEM] + [VMEM] * 5 + [ANY] * len(blocks) + [VMEM],
            out_specs=VMEM,
            out_shape=near(acc_shape, F32),
            input_output_aliases={6 + len(blocks): 0},
            scratch_shapes=[
                pltpu.VMEM((len(blocks), TOK, C), BF16),
                pltpu.SemaphoreType.DMA((len(blocks),)),
            ],
            compiler_params=params(28),
            cost_estimate=cost(3.5 * len(rows)),
        )(rows_place(rows), affine, query, top, wk, wv_t, *blocks, acc)

    query, acc, top = pl.pallas_call(
        open_kernel,
        in_specs=[SMEM] + [VMEM] * 6,
        out_specs=[VMEM] * 3,
        out_shape=[
            near((MINE, 2 * HEAD_DIM, QUERIES), BF16),
            near(acc_shape, F32),
            near((MINE, 8, QUERIES), F32),
        ],
        compiler_params=params(28),
        cost_estimate=cost(0),
    )(rows_place(mine[0] + theirs[0]), affine, resid, other_0, wq_t, wk, wv_t)

    c_far = send(c_up, Z_UP)
    d_up = send(c_up, X_LO)
    d_down = send(d_own, Z_DOWN)
    mine_1 = [c_up, c_down, d_own]
    other_1 = [send(c_up, SIBLING)]
    acc = attend(mine_1, mine[1], acc)
    late, other_1, acc = lax.optimization_barrier((mine_1[1:], other_1, acc))
    other_1 += [send(block, pairs) for block, pairs in zip(late, SIBLINGS)]
    acc = attend(other_1[:1], theirs[1][:1], acc)
    c_far, d_up, d_down, other_1, acc = lax.optimization_barrier(
        (c_far, d_up, d_down, other_1, acc)
    )
    last = send(c_far, X_LO)
    mine_2 = [c_far, d_up, d_down]
    other_2 = [send(block, pairs) for block, pairs in zip(mine_2, SIBLINGS)]
    acc = attend(other_1[1:], theirs[1][1:], acc)
    acc = attend(mine_2, mine[2], acc)
    last, other_2, acc = lax.optimization_barrier((last, other_2, acc))
    other_3 = send(last, SIBLING)
    acc = attend(other_2 + [last], theirs[2] + mine[3], acc)
    other_3, acc = lax.optimization_barrier((other_3, acc))
    blocks = [resid, other_0] + mine_1 + other_1 + mine_2 + other_2 + [last, other_3]
    order = mine[0] + theirs[0] + mine[1] + theirs[1] + mine[2] + theirs[2] + mine[3] + theirs[3]
    mixed, others = pl.pallas_call(
        close_kernel,
        in_specs=[SMEM] + [VMEM] * 7 + [ANY] * 16,
        out_specs=[VMEM] * 2,
        out_shape=[near((HALF_C, TOK), BF16)] * 2,
        scratch_shapes=[
            pltpu.VMEM(acc_shape, F32),
            pltpu.VMEM((MINE, 1, QUERIES), F32),
            pltpu.VMEM((TOK, C), BF16),
            pltpu.SemaphoreType.DMA,
        ],
        compiler_params=params(28),
        cost_estimate=cost(5),
    )(rows_place(order), affine, query, top, wk, wv_t, other_3, acc, *blocks)
    other = send(others, SIBLING)
    out = pl.pallas_call(
        finish_kernel,
        in_specs=[SMEM] + [VMEM] * 5,
        out_specs=VMEM,
        out_shape=shape((TOK, C), BF16),
        compiler_params=params(20),
    )(place, mixed, other, resid, out_weight, out_bias[None, :])
    return out.reshape(1, RP, W, C)


def solution(mesh):
    in_specs = (
        P("image", "patch", None, None),
        P("image"),
        P(),
        P(),
        P(None, None, "image", None),
        P(),
        P(),
        P(),
        P(),
        P(),
        P(),
        P(),
        P(),
    )
    out_specs = P("image", "patch", None, None)
    return jax.shard_map(
        per_device, mesh=mesh, in_specs=in_specs, out_specs=out_specs, check_vma=False
    )
```

time: 449 us -> 272 us (0.61)
  Pallas kernels: 0 us -> 181 us
  matrix products: 135 us -> 0 us
  blocking collectives: 117 us -> 0 us
  other arithmetic: 58.9 us -> 1.28 us
  waiting for transfers between devices: 84.4 us -> 28.5 us
  starting transfers between devices: 4.61 us -> 44.7 us
  local copies, waits for them, and re-layouts: 34.2 us -> 9.68 us
  between operations: 14.2 us -> 1.6 us
    pallas_call x0 -> x15, Pallas kernels: none -> 181 us  [the longest x1 94.6 us: per_device(): pl.pallas_call(close_kernel, in_specs=[SMEM] + [VMEM] * 7 + [ANY] * 16, o...]
    dot_general x15 -> x0, matrix products: 135 us -> none  [the longest x1 60.9 us: per_device(): jnp.einsum('qhd,khd->hqk', query_heads, absorb_keys.reshape(count_k, head...]
    psum x4 -> x0, blocking collectives: 117 us -> none  [the longest x2 59.7 us: normalize_rows(): lax.psum(jnp.sum(centred * centred, axis=(0, 1, 3)), 'patch')]
    all_gather x3 -> x0, waiting for transfers between devices: 81.5 us -> none  [the longest x1 54.8 us: per_device(): absorb_keys = lax.all_gather(keys, 'patch', axis=0, tiled=True)]
    reduce_sum x8, other arithmetic: 52.5 us -> 0.98 us  [the longest x4 0.54 us: combine(): spread = jnp.sum(squares + counts * apart * apart, axis=(0, 2)) / entries]
    all_gather x2 -> x0, local copies, waits for them, and re-layouts: 28.9 us -> none  [the longest x1 14.5 us: per_device(): absorb_values = lax.all_gather(values, 'patch', axis=0, tiled=True)]
    ppermute x2 -> x32, starting transfers between devices: 4.32 us -> 31.5 us  [send(): return lax.ppermute(block, BOTH, pairs)]
    all_to_all x0 -> x2, waiting for transfers between devices: none -> 17.8 us  [exchange(): return lax.all_to_all(stats, 'patch', 0, 0, tiled=False)]
  transfers between devices with their start and end apart: 5 -> 34, of which waited for: 3 -> 5; matrix products, arithmetic and copies ran while one was open for 31% -> 1% of each run, Pallas kernels for 0% -> 30%
where the time goes in v2:
time: 272 us; the launch traced here: 267 us
  Pallas kernels  181 us (67%)
  starting transfers between devices  44.7 us (16%)
  waiting for transfers between devices  28.5 us (10%)
  local copies, waits for them, and re-layouts  9.68 us (4%)
    pallas_call x1, Pallas kernels, per_device(): pl.pallas_call(close_kernel, in_specs=[SMEM] + [VMEM] * 7 + [ANY] * 16, o...  94.6 us
    pallas_call x5, Pallas kernels, attend(): pl.pallas_call(functools.partial(attend_kernel, len(blocks)), in_specs=[S...  48.6 us
    ppermute x32, starting transfers between devices, send(): return lax.ppermute(block, BOTH, pairs)  31.5 us
    all_to_all x2, waiting for transfers between devices, exchange(): return lax.all_to_all(stats, 'patch', 0, 0, tiled=False)  17.8 us
    pallas_call x1, Pallas kernels, per_device(): pl.pallas_call(conv_open_kernel, in_specs=[SMEM] + [VMEM] * 8, out_specs=...  14.8 us
    all_to_all x2, starting transfers between devices, exchange(): return lax.all_to_all(stats, 'patch', 0, 0, tiled=False)  13.2 us
    ppermute x32, waiting for transfers between devices, send(): return lax.ppermute(block, BOTH, pairs)  10.6 us
    pallas_call x1, Pallas kernels, per_device(): pl.pallas_call(open_kernel, in_specs=[SMEM] + [VMEM] * 6, out_specs=[VMEM...  8.31 us
  transfers between devices with their start and end apart: 34, of which 5 were waited for; matrix products, arithmetic and copies ran while one was open for 1% of the time, Pallas kernels for 30%

profile of v2, /device:TPU:1, one launch (start us, length us, event | category | flops | bytes accessed | tf_op | source)
XLA Modules:
  0.0 267.0 jit_solution(16213396202292502742)
XLA Ops:
  2.9 3.4 %collective-permute-start.2 = (bf16[368,640]{1,0:T(8,128)(2,1)S(1)}, bf16[368,640]{1,0:T(8,128)(2,1)S(1)}, u32[]{:S(2)}, u32[]{:S(2)}) collective-permute-start(bf16[368,640]{1,0:T(8,128)(2,1)S(1)} %shard_map.127), channel_id=1, source_target_pairs={{0,72},{1,73},{2,74},{3,75},{4,76},{5,77},{6,78},{7,79},{16,88},{1... | collective-permute-start | bytes 1413128 | tf_op jit(solution)/shard_map/ppermute | solution.py:75
  6.2 2.7 %collective-permute-start.1 = (bf16[368,640]{1,0:T(8,128)(2,1)S(1)}, bf16[368,640]{1,0:T(8,128)(2,1)S(1)}, u32[]{:S(2)}, u32[]{:S(2)}) collective-permute-start(bf16[368,640]{1,0:T(8,128)(2,1)S(1)} %shard_map.127), channel_id=1, source_target_pairs={{0,48},{1,49},{2,50},{3,51},{4,52},{5,53},{6,54},{7,55},{16,0},{17... | collective-permute-start | bytes 1413128 | tf_op jit(solution)/shard_map/ppermute | solution.py:75
  10.7 6.6 %all-to-all-start = ((f32[16,2,640]{2,1,0:T(2,128)}), f32[16,2,640]{2,1,0:T(2,128)S(1)}, u32[]{:S(2)}, u32[]{:S(2)}) async-start(f32[16,2,640]{2,1,0:T(2,128)} %shard_map.128), calls=%async_computation | async-start | bytes 163840 | tf_op jit(solution)/shard_map/all_to_all | solution.py:410
  17.3 5.8 %all-to-all-done = f32[16,2,640]{2,1,0:T(2,128)S(1)} async-done(((f32[16,2,640]{2,1,0:T(2,128)}), f32[16,2,640]{2,1,0:T(2,128)S(1)}, u32[]{:S(2)}, u32[]{:S(2)}) %all-to-all-start) | async-done | bytes 81952 | tf_op jit(solution)/shard_map/all_to_all | solution.py:410
  24.1 3.0 %collective-permute-start.5 = (bf16[368,640]{1,0:T(8,128)(2,1)S(1)}, bf16[368,640]{1,0:T(8,128)(2,1)S(1)}, u32[]{:S(2)}, u32[]{:S(2)}) collective-permute-start(bf16[368,640]{1,0:T(8,128)(2,1)S(1)} %collective-permute-done.2.c), channel_id=1, source_target_pairs={{0,48},{1,49},{2,50},{3,51},{4,52},{5,53},{6,54},{7,55},{16,0},{17... | collective-permute-start | bytes 1413128 | tf_op jit(solution)/shard_map/ppermute | solution.py:75
  27.4 2.8 %collective-permute-start.6 = (bf16[64,640]{1,0:T(8,128)(2,1)S(1)}, bf16[64,640]{1,0:T(8,128)(2,1)S(1)}, u32[]{:S(2)}, u32[]{:S(2)}) collective-permute-start(bf16[64,640]{1,0:T(8,128)(2,1)S(1)} %get-tuple-element.76), channel_id=1, source_target_pairs={{0,1},{1,2},{2,3},{3,4},{4,5},{5,6},{6,7},{7,8},{8,9},{9,10},{10,1... | collective-permute-start | bytes 245768 | tf_op jit(solution)/shard_map/ppermute | solution.py:75
  32.5 3.7 %collective-permute-done.7.below_ref = bf16[64,640]{1,0:T(8,128)(2,1)S(1)} collective-permute-done((bf16[64,640]{1,0:T(8,128)(2,1)S(1)}, bf16[64,640]{1,0:T(8,128)(2,1)S(1)}, u32[]{:S(2)}, u32[]{:S(2)}) %collective-permute-start.7) | collective-permute-done | bytes 81952 | tf_op jit(solution)/shard_map/ppermute | solution.py:75
  39.3 5.4 %collective-permute-done.4.b = bf16[368,640]{1,0:T(8,128)(2,1)S(1)} collective-permute-done((bf16[368,640]{1,0:T(8,128)(2,1)S(1)}, bf16[368,640]{1,0:T(8,128)(2,1)S(1)}, u32[]{:S(2)}, u32[]{:S(2)}) %collective-permute-start.4) | collective-permute-done | bytes 471072 | tf_op jit(solution)/shard_map/ppermute | solution.py:75
  47.0 2.4 collective-permute-start.11
  49.9 14.8 %shard_map.130.held_ref = f32[512,640]{1,0:T(8,128)S(1)} custom-call(s32[11]{0:T(128)S(1)} %stack.152.place_ref, bf16[640,384]{1,0:T(8,128)(2,1)S(1)} %get-tuple-element.91.first_ref, bf16[720,640]{1,0:T(8,128)(2,1)S(1)} %bitcast.40, bf16[368,640]{1,0:T(8,128)(2,1)S(1)} %collective-permute-done.a, bf16[368,640]{1,0:T(8,128)(2,1)S(1)} %collective-permute-done.1.b, ...), custom_call_target="tpu_custom_call" | custom-call | flops 5000000000 | bytes 15000000 | tf_op jit(solution)/shard_map/pallas_call | solution.py:513
  66.7 2.7 %shard_map.132.held_ref = f32[512,640]{1,0:T(8,128)S(1)} custom-call(s32[11]{0:T(128)S(1)} %stack.152.place_ref, bf16[640,256]{1,0:T(8,128)(2,1)S(1)} %get-tuple-element.103.first_ref, bf16[368,640]{1,0:T(8,128)(2,1)S(1)} %collective-permute-done.3.a, bf16[368,640]{1,0:T(8,128)(2,1)S(1)} %collective-permute-done.4.b, ...), custom_call_target="tpu_custom_call", output_to_operand_aliasing={{}: (8, {})} | custom-call | flops 4000000000 | bytes 12000000 | tf_op jit(solution)/shard_map/pallas_call | solution.py:534
  69.5 3.7 %shard_map.133 = (bf16[512,640]{1,0:T(8,128)(2,1)S(1)}, f32[16,2,640]{2,1,0:T(2,128)}) custom-call(s32[11]{0:T(128)S(1)} %stack.152.place_ref, bf16[640,128]{1,0:T(8,128)(2,1)S(1)} %get-tuple-element.87.first_ref, bf16[368,640]{1,0:T(8,128)(2,1)S(1)} %collective-permute-done.11.a, bf16[368,640]{1,0:T(8,128)(2,1)S(1)} %collective-permute-done.15.theirs_ref, ...), custom_call_target="tpu_custom_call" | custom-call | tf_op jit(solution)/shard_map/pallas_call | solution.py:544
  73.4 2.5 collective-permute-start.17
  76.0 6.6 %all-to-all-start.1 = ((f32[16,2,640]{2,1,0:T(2,128)}), f32[16,2,640]{2,1,0:T(2,128)S(1)}, u32[]{:S(2)}, u32[]{:S(2)}) async-start(f32[16,2,640]{2,1,0:T(2,128)} %get-tuple-element.109), calls=%async_computation.1 | async-start | bytes 163840 | tf_op jit(solution)/shard_map/all_to_all | solution.py:410
  82.7 12.1 %all-to-all-done.1 = f32[16,2,640]{2,1,0:T(2,128)S(1)} async-done(((f32[16,2,640]{2,1,0:T(2,128)}), f32[16,2,640]{2,1,0:T(2,128)S(1)}, u32[]{:S(2)}, u32[]{:S(2)}) %all-to-all-start.1) | async-done | bytes 81952 | tf_op jit(solution)/shard_map/all_to_all | solution.py:410
  98.0 3.0 %collective-permute-start.22 = (bf16[512,640]{1,0:T(8,128)(2,1)S(1)}, bf16[512,640]{1,0:T(8,128)(2,1)}, u32[]{:S(2)}, u32[]{:S(2)}) collective-permute-start(bf16[512,640]{1,0:T(8,128)(2,1)S(1)} %collective-permute-done.18.refs_2_.refs_4_), channel_id=1, source_target_pairs={{0,6},{1,7},{2,0},{3,1},{4,2},{5,3},{6,4},{7,5},{16,22},{17,23},{1... | collective-permute-start | bytes 1966088 | tf_op jit(solution)/shard_map/ppermute | solution.py:75
  100.9 8.3 %shard_map.134 = (bf16[5,128,1024]{2,1,0:T(8,128)(2,1)S(1)}, f32[5,80,1024]{2,1,0:T(8,128)S(1)}, f32[5,8,1024]{2,1,0:T(8,128)S(1)}) custom-call(s32[4]{0:T(128)S(1)} %pad_add_fusion.place_ref, f32[3,640]{1,0:T(4,128)S(1)} %pad_maximum_fusion.1.affine_ref, bf16[512,640]{1,0:T(8,128)(2,1)S(1)} %get-tuple-element.108.own_ref.refs_0_.resid_ref, ...), custom_call_target="tpu_custom_call" | custom-call | tf_op jit(solution)/shard_map/pallas_call | solution.py:591
  109.3 11.0 %shard_map.135.refs_1_ = f32[5,80,1024]{2,1,0:T(8,128)S(1)} custom-call(s32[5]{0:T(128)S(1)} %stack.177.place_ref, f32[3,640]{1,0:T(4,128)S(1)} %pad_maximum_fusion.1.affine_ref, bf16[5,128,1024]{2,1,0:T(8,128)(2,1)S(1)} %get-tuple-element.115.query_ref, f32[5,8,1024]{2,1,0:T(8,128)S(1)} %get-tuple-element.116.top_ref, ...), custom_call_target="tpu_custom_call", output_to_operand_aliasing={{}: (9, {})} | custom-call | flops 10499999744 | bytes 31500000 | tf_op jit(solution)/shard_map/pallas_call | solution.py:577
  126.1 4.7 %shard_map.136.refs_2_ = f32[5,80,1024]{2,1,0:T(8,128)S(1)} custom-call(s32[3]{0:T(128)S(1)} %pad_add_fusion.2.place_ref, f32[3,640]{1,0:T(4,128)S(1)} %pad_maximum_fusion.1.affine_ref, bf16[5,128,1024]{2,1,0:T(8,128)(2,1)S(1)} %copy-done.9, f32[5,8,1024]{2,1,0:T(8,128)S(1)} %get-tuple-element.116.top_ref, ...), custom_call_target="tpu_custom_call", output_to_operand_aliasing={{}: (7, {})} | custom-call | flops 3500000000 | bytes 10500000 | tf_op jit(solution)/shard_map/pallas_call | solution.py:577
  131.9 7.9 %shard_map.137.refs_3_ = f32[5,80,1024]{2,1,0:T(8,128)S(1)} custom-call(s32[4]{0:T(128)S(1)} %pad_add_fusion.3.place_ref, f32[3,640]{1,0:T(4,128)S(1)} %pad_maximum_fusion.1.affine_ref, bf16[5,128,1024]{2,1,0:T(8,128)(2,1)S(1)} %copy-done.9, f32[5,8,1024]{2,1,0:T(8,128)S(1)} %get-tuple-element.116.top_ref, ...), custom_call_target="tpu_custom_call", output_to_operand_aliasing={{}: (8, {})} | custom-call | flops 7000000000 | bytes 21000000 | tf_op jit(solution)/shard_map/pallas_call | solution.py:577
  139.8 11.0 %shard_map.138.refs_4_ = f32[5,80,1024]{2,1,0:T(8,128)S(1)} custom-call(s32[5]{0:T(128)S(1)} %stack.179.place_ref, f32[3,640]{1,0:T(4,128)S(1)} %pad_maximum_fusion.1.affine_ref, bf16[5,128,1024]{2,1,0:T(8,128)(2,1)S(1)} %copy-done.9, f32[5,8,1024]{2,1,0:T(8,128)S(1)} %get-tuple-element.116.top_ref, ...), custom_call_target="tpu_custom_call", output_to_operand_aliasing={{}: (9, {})} | custom-call | flops 10499999744 | bytes 31500000 | tf_op jit(solution)/shard_map/pallas_call | solution.py:577
  151.4 14.0 %shard_map.139.held_ref = f32[5,80,1024]{2,1,0:T(8,128)S(1)} custom-call(s32[6]{0:T(128)S(1)} %stack.181.place_ref, f32[3,640]{1,0:T(4,128)S(1)} %pad_maximum_fusion.1.affine_ref, bf16[5,128,1024]{2,1,0:T(8,128)(2,1)S(1)} %copy-done.9, f32[5,8,1024]{2,1,0:T(8,128)S(1)} %get-tuple-element.116.top_ref, ...), custom_call_target="tpu_custom_call", output_to_operand_aliasing={{}: (10, {})} | custom-call | flops 14000000000 | bytes 42000000 | tf_op jit(solution)/shard_map/pallas_call | solution.py:577
  168.2 94.6 %shard_map.140 = (bf16[320,512]{1,0:T(8,128)(2,1)S(1)}, bf16[320,512]{1,0:T(8,128)(2,1)S(1)}) custom-call(s32[18]{0:T(128)S(1)} %stack.169.place_ref, f32[3,640]{1,0:T(4,128)S(1)} %pad_maximum_fusion.1.affine_ref, bf16[5,128,1024]{2,1,0:T(8,128)(2,1)S(1)} %copy-done.9, f32[5,8,1024]{2,1,0:T(8,128)S(1)} %get-tuple-element.116.top_ref, ...), custom_call_target="tpu_custom_call" | custom-call | flops 5000000000 | bytes 15000000 | tf_op jit(solution)/shard_map/pallas_call | solution.py:627
  264.5 2.3 shard_map.141
  (143 shorter events, 30.5 us)
Async XLA Ops:
  2.9 21.2 %collective-permute-start.2 = (bf16[368,640]{1,0:T(8,128)(2,1)S(1)}, bf16[368,640]{1,0:T(8,128)(2,1)S(1)}, u32[]{:S(2)}, u32[]{:S(2)}) collective-permute-start(bf16[368,640]{1,0:T(8,128)(2,1)S(1)} %shard_map.127), channel_id=1, source_target_pairs={{0,72},{1,73},{2,74},{3,75},{4,76},{5,77},{6,78},{7,79},{16,88},{1... | collective-permute-start | bytes 1413128 | tf_op jit(solution)/shard_map/ppermute | solution.py:75
  6.2 17.8 %collective-permute-start.1 = (bf16[368,640]{1,0:T(8,128)(2,1)S(1)}, bf16[368,640]{1,0:T(8,128)(2,1)S(1)}, u32[]{:S(2)}, u32[]{:S(2)}) collective-permute-start(bf16[368,640]{1,0:T(8,128)(2,1)S(1)} %shard_map.127), channel_id=1, source_target_pairs={{0,48},{1,49},{2,50},{3,51},{4,52},{5,53},{6,54},{7,55},{16,0},{17... | collective-permute-start | bytes 1413128 | tf_op jit(solution)/shard_map/ppermute | solution.py:75
  9.0 15.1 %collective-permute-start = (bf16[368,640]{1,0:T(8,128)(2,1)S(1)}, bf16[368,640]{1,0:T(8,128)(2,1)S(1)}, u32[]{:S(2)}, u32[]{:S(2)}) collective-permute-start(bf16[368,640]{1,0:T(8,128)(2,1)S(1)} %shard_map.127), channel_id=1, source_target_pairs={{0,16},{1,17},{2,18},{3,19},{4,20},{5,21},{6,22},{7,23},{16,32},{1... | collective-permute-start | bytes 1413128 | tf_op jit(solution)/shard_map/ppermute | solution.py:75
  10.7 12.4 %all-to-all-start = ((f32[16,2,640]{2,1,0:T(2,128)}), f32[16,2,640]{2,1,0:T(2,128)S(1)}, u32[]{:S(2)}, u32[]{:S(2)}) async-start(f32[16,2,640]{2,1,0:T(2,128)} %shard_map.128), calls=%async_computation | async-start | bytes 163840 | tf_op jit(solution)/shard_map/all_to_all | solution.py:410
  24.1 15.0 %collective-permute-start.5 = (bf16[368,640]{1,0:T(8,128)(2,1)S(1)}, bf16[368,640]{1,0:T(8,128)(2,1)S(1)}, u32[]{:S(2)}, u32[]{:S(2)}) collective-permute-start(bf16[368,640]{1,0:T(8,128)(2,1)S(1)} %collective-permute-done.2.c), channel_id=1, source_target_pairs={{0,48},{1,49},{2,50},{3,51},{4,52},{5,53},{6,54},{7,55},{16,0},{17... | collective-permute-start | bytes 1413128 | tf_op jit(solution)/shard_map/ppermute | solution.py:75
  32.1 12.5 %collective-permute-start.4 = (bf16[368,640]{1,0:T(8,128)(2,1)S(1)}, bf16[368,640]{1,0:T(8,128)(2,1)S(1)}, u32[]{:S(2)}, u32[]{:S(2)}) collective-permute-start(bf16[368,640]{1,0:T(8,128)(2,1)S(1)} %collective-permute-done.a), channel_id=1, source_target_pairs={{0,72},{1,73},{2,74},{3,75},{4,76},{5,77},{6,78},{7,79},{16,88},{1... | collective-permute-start | bytes 1413128 | tf_op jit(solution)/shard_map/ppermute | solution.py:75
  44.7 21.6 %collective-permute-start.12 = (bf16[368,640]{1,0:T(8,128)(2,1)S(1)}, bf16[368,640]{1,0:T(8,128)(2,1)S(1)}, u32[]{:S(2)}, u32[]{:S(2)}) collective-permute-start(bf16[368,640]{1,0:T(8,128)(2,1)S(1)} %collective-permute-done.3.a), channel_id=1, source_target_pairs={{0,1},{1,0},{2,3},{3,2},{4,5},{5,4},{6,7},{7,6},{16,17},{17,16},{1... | collective-permute-start | bytes 1413128 | tf_op jit(solution)/shard_map/ppermute | solution.py:75
  47.0 19.3 %collective-permute-start.11 = (bf16[368,640]{1,0:T(8,128)(2,1)S(1)}, bf16[368,640]{1,0:T(8,128)(2,1)S(1)}, u32[]{:S(2)}, u32[]{:S(2)}) collective-permute-start(bf16[368,640]{1,0:T(8,128)(2,1)S(1)} %collective-permute-done.3.a), channel_id=1, source_target_pairs={{0,72},{1,73},{2,74},{3,75},{4,76},{5,77},{6,78},{7,79},{16,88},{1... | collective-permute-start | bytes 1413128 | tf_op jit(solution)/shard_map/ppermute | solution.py:75
  49.4 16.8 %collective-permute-start.13 = (bf16[368,640]{1,0:T(8,128)(2,1)S(1)}, bf16[368,640]{1,0:T(8,128)(2,1)S(1)}, u32[]{:S(2)}, u32[]{:S(2)}) collective-permute-start(bf16[368,640]{1,0:T(8,128)(2,1)S(1)} %collective-permute-done.4.b), channel_id=1, source_target_pairs={{1,0},{2,3},{3,2},{4,5},{5,4},{6,7},{7,6},{16,17},{17,16},{18,19},... | collective-permute-start | bytes 1413128 | tf_op jit(solution)/shard_map/ppermute | solution.py:75
  49.8 16.5 %collective-permute-start.14 = (bf16[368,640]{1,0:T(8,128)(2,1)S(1)}, bf16[368,640]{1,0:T(8,128)(2,1)S(1)}, u32[]{:S(2)}, u32[]{:S(2)}) collective-permute-start(bf16[368,640]{1,0:T(8,128)(2,1)S(1)} %collective-permute-done.5.c), channel_id=1, source_target_pairs={{2,3},{3,2},{4,5},{5,4},{6,7},{7,6},{16,17},{17,16},{18,19},{19,18... | collective-permute-start | bytes 1413128 | tf_op jit(solution)/shard_map/ppermute | solution.py:75
  73.2 21.5 %collective-permute-start.19 = (bf16[512,640]{1,0:T(8,128)(2,1)S(1)}, bf16[512,640]{1,0:T(8,128)(2,1)S(1)}, u32[]{:S(2)}, u32[]{:S(2)}) collective-permute-start(bf16[512,640]{1,0:T(8,128)(2,1)S(1)} %get-tuple-element.108.own_ref.refs_0_.resid_ref), channel_id=1, source_target_pairs={{0,1},{1,0},{2,3},{3,2},{4,5},{5,4},{6,7},{7,6},{16,17},{17,16},{1... | collective-permute-start | bytes 1966088 | tf_op jit(solution)/shard_map/ppermute | solution.py:75
  73.4 21.3 %collective-permute-start.18 = (bf16[512,640]{1,0:T(8,128)(2,1)S(1)}, bf16[512,640]{1,0:T(8,128)(2,1)S(1)}, u32[]{:S(2)}, u32[]{:S(2)}) collective-permute-start(bf16[512,640]{1,0:T(8,128)(2,1)S(1)} %get-tuple-element.108.own_ref.refs_0_.resid_ref), channel_id=1, source_target_pairs={{0,8},{1,9},{2,10},{3,11},{4,12},{5,13},{6,14},{7,15},{16,24},{17,... | collective-permute-start | bytes 1966088 | tf_op jit(solution)/shard_map/ppermute | solution.py:75
  73.4 21.3 %collective-permute-start.17 = (bf16[512,640]{1,0:T(8,128)(2,1)S(1)}, bf16[512,640]{1,0:T(8,128)(2,1)}, u32[]{:S(2)}, u32[]{:S(2)}) collective-permute-start(bf16[512,640]{1,0:T(8,128)(2,1)S(1)} %get-tuple-element.108.own_ref.refs_0_.resid_ref), channel_id=1, source_target_pairs={{0,6},{1,7},{2,0},{3,1},{4,2},{5,3},{6,4},{7,5},{16,22},{17,23},{1... | collective-permute-start | bytes 1966088 | tf_op jit(solution)/shard_map/ppermute | solution.py:75
  75.9 18.9 %collective-permute-start.16 = (bf16[512,640]{1,0:T(8,128)(2,1)S(1)}, bf16[512,640]{1,0:T(8,128)(2,1)}, u32[]{:S(2)}, u32[]{:S(2)}) collective-permute-start(bf16[512,640]{1,0:T(8,128)(2,1)S(1)} %get-tuple-element.108.own_ref.refs_0_.resid_ref), channel_id=1, source_target_pairs={{0,2},{1,3},{2,4},{3,5},{4,6},{5,7},{6,0},{7,1},{16,18},{17,19},{1... | collective-permute-start | bytes 1966088 | tf_op jit(solution)/shard_map/ppermute | solution.py:75
  76.0 18.7 %all-to-all-start.1 = ((f32[16,2,640]{2,1,0:T(2,128)}), f32[16,2,640]{2,1,0:T(2,128)S(1)}, u32[]{:S(2)}, u32[]{:S(2)}) async-start(f32[16,2,640]{2,1,0:T(2,128)} %get-tuple-element.109), calls=%async_computation.1 | async-start | bytes 163840 | tf_op jit(solution)/shard_map/all_to_all | solution.py:410
  95.4 26.0 %collective-permute-start.23 = (bf16[512,640]{1,0:T(8,128)(2,1)}, bf16[512,640]{1,0:T(8,128)(2,1)}, u32[]{:S(2)}, u32[]{:S(2)}) collective-permute-start(bf16[512,640]{1,0:T(8,128)(2,1)} %collective-permute-done.16.refs_0_.refs_2_), channel_id=1, source_target_pairs={{0,1},{1,0},{2,3},{3,2},{4,5},{5,4},{6,7},{7,6},{16,17},{17,16},{1... | collective-permute-start | bytes 1966088 | tf_op jit(solution)/shard_map/ppermute | solution.py:75
  95.9 34.9 %collective-permute-start.21 = (bf16[512,640]{1,0:T(8,128)(2,1)}, bf16[512,640]{1,0:T(8,128)(2,1)}, u32[]{:S(2)}, u32[]{:S(2)}) collective-permute-start(bf16[512,640]{1,0:T(8,128)(2,1)} %collective-permute-done.16.refs_0_.refs_2_), channel_id=1, source_target_pairs={{0,8},{1,9},{2,10},{3,11},{4,12},{5,13},{6,14},{7,15},{16,24},{17,... | collective-permute-start | bytes 1966088 | tf_op jit(solution)/shard_map/ppermute | solution.py:75
  97.3 33.5 %collective-permute-start.20 = (bf16[512,640]{1,0:T(8,128)(2,1)}, bf16[512,640]{1,0:T(8,128)(2,1)}, u32[]{:S(2)}, u32[]{:S(2)}) collective-permute-start(bf16[512,640]{1,0:T(8,128)(2,1)} %collective-permute-done.16.refs_0_.refs_2_), channel_id=1, source_target_pairs={{0,2},{1,3},{2,4},{3,5},{4,6},{5,7},{6,0},{7,1},{16,18},{17,19},{1... | collective-permute-start | bytes 1966088 | tf_op jit(solution)/shard_map/ppermute | solution.py:75
  98.0 32.9 %collective-permute-start.22 = (bf16[512,640]{1,0:T(8,128)(2,1)S(1)}, bf16[512,640]{1,0:T(8,128)(2,1)}, u32[]{:S(2)}, u32[]{:S(2)}) collective-permute-start(bf16[512,640]{1,0:T(8,128)(2,1)S(1)} %collective-permute-done.18.refs_2_.refs_4_), channel_id=1, source_target_pairs={{0,6},{1,7},{2,0},{3,1},{4,2},{5,3},{6,4},{7,5},{16,22},{17,23},{1... | collective-permute-start | bytes 1966088 | tf_op jit(solution)/shard_map/ppermute | solution.py:75
  130.9 19.9 %collective-permute-start.27 = (bf16[512,640]{1,0:T(8,128)(2,1)}, bf16[512,640]{1,0:T(8,128)(2,1)S(1)}, u32[]{:S(2)}, u32[]{:S(2)}) collective-permute-start(bf16[512,640]{1,0:T(8,128)(2,1)} %collective-permute-done.20.refs_0_.refs_8_), channel_id=1, source_target_pairs={{0,1},{1,0},{2,3},{3,2},{4,5},{5,4},{6,7},{7,6},{16,17},{17,16},{1... | collective-permute-start | bytes 1966088 | tf_op jit(solution)/shard_map/ppermute | solution.py:75
  131.4 19.4 %collective-permute-start.26 = (bf16[512,640]{1,0:T(8,128)(2,1)}, bf16[512,640]{1,0:T(8,128)(2,1)S(1)}, u32[]{:S(2)}, u32[]{:S(2)}) collective-permute-start(bf16[512,640]{1,0:T(8,128)(2,1)} %collective-permute-done.20.refs_0_.refs_8_), channel_id=1, source_target_pairs={{0,8},{1,9},{2,10},{3,11},{4,12},{5,13},{6,14},{7,15},{16,24},{17,... | collective-permute-start | bytes 1966088 | tf_op jit(solution)/shard_map/ppermute | solution.py:75
  131.4 19.4 %collective-permute-start.28 = (bf16[512,640]{1,0:T(8,128)(2,1)}, bf16[512,640]{1,0:T(8,128)(2,1)S(1)}, u32[]{:S(2)}, u32[]{:S(2)}) collective-permute-start(bf16[512,640]{1,0:T(8,128)(2,1)} %collective-permute-done.21.refs_1_.refs_9_), channel_id=1, source_target_pairs={{1,0},{2,3},{3,2},{4,5},{5,4},{6,7},{7,6},{16,17},{17,16},{18,19},... | collective-permute-start | bytes 1966088 | tf_op jit(solution)/shard_map/ppermute | solution.py:75
  131.8 19.0 %collective-permute-start.29 = (bf16[512,640]{1,0:T(8,128)(2,1)}, bf16[512,640]{1,0:T(8,128)(2,1)S(1)}, u32[]{:S(2)}, u32[]{:S(2)}) collective-permute-start(bf16[512,640]{1,0:T(8,128)(2,1)} %collective-permute-done.22.refs_2_.refs_10_), channel_id=1, source_target_pairs={{2,3},{3,2},{4,5},{5,4},{6,7},{7,6},{16,17},{17,16},{18,19},{19,18... | collective-permute-start | bytes 1966088 | tf_op jit(solution)/shard_map/ppermute | solution.py:75
  150.8 15.9 %collective-permute-start.30 = (bf16[512,640]{1,0:T(8,128)(2,1)S(1)}, bf16[512,640]{1,0:T(8,128)(2,1)S(1)}, u32[]{:S(2)}, u32[]{:S(2)}) collective-permute-start(bf16[512,640]{1,0:T(8,128)(2,1)S(1)} %collective-permute-done.26.refs_3_.refs_14_), channel_id=1, source_target_pairs={{0,1},{1,0},{2,3},{3,2},{4,5},{5,4},{6,7},{7,6},{16,17},{17,16},{1... | collective-permute-start | bytes 1966088 | tf_op jit(solution)/shard_map/ppermute | solution.py:75
  (29 other events, 458.7 us)
